TPU v7x, 32 devices: a whole 2x2x4 slice. The times are simulated.
32 devices in a mesh: tm: 8 (over z, x), col: 4 (over y, core).
Axes of the slice: x: 2, y: 2, z: 4, core: 2. Of those that a mesh axis runs over, the one named last changes fastest.
Arguments:
- observations: float32 [128, 64, 256], P('tm', 'col'), may hold values from -6 to 6
- band_index: int32 [128], P('tm'), may hold values from 0 to 3
- obs_mask: int32 [128], P('tm'), may hold values 0 or 1
- diffusivity: float32 [4, 256], replicated, may hold values from 0.005 to 0.05
- mode_correction_factors: float32 [4, 256, 256], replicated, may hold values from -0.01 to 0.06
- mode_backward_factors: float32 [4, 256, 256], replicated, may hold values from -0.01 to 1.01
- initial_mean: float32 [256], replicated, may hold values from -6 to 6
Outputs:
- filtered: float32 [128, 64, 256], P('tm', 'col')
- smoothed: float32 [128, 64, 256], P('tm', 'col')
All inputs are finite; a program needn't handle non-finite values. No bound on the sum of `obs_mask` on one device may be relied on, other than what follows from the above.
Results may differ from a plain program's by a relative error of at most 0.0003.
Values sent between devices are 32-bit elements; how exact they have to be, the bound alone decides.
No kernel may reach another device: no remote copies, remote signals or barrier semaphores. Data moves between devices by JAX's collectives and lax.ppermute only.
A program may use at most 64 MiB of HBM per device.

v0:
```python
import functools

import jax
import jax.numpy as jnp
from jax import lax
from jax.experimental import pallas as pl
from jax.experimental.pallas import tpu as pltpu
from jax.sharding import PartitionSpec as P

GRID = 16
SLOTS = 3
META = 8
MASK_AT, SLOT_AT, COUNT_AT = 32, 64, 96
BF, F32 = jnp.bfloat16, jnp.float32
VMEM_BYTES = 24 * 2**20
PACK_VMEM_BYTES = 60 * 2**20


def halves(value):
    high = value.astype(BF)
    return high, (value - high.astype(F32)).astype(BF)


def dot(a, b):
    return jnp.dot(a, b, preferred_element_type=F32)


def rows_product(rows, high, low):
    m = rows.shape[0]
    rows_high, rows_low = halves(rows)
    both = dot(jnp.concatenate([rows_high, rows_low], 0), high)
    return both[:m] + both[m:] + dot(rows_high, low)


def from_cell(value, shift):
    cells = value.shape[-1]
    return pltpu.roll(value, (-shift) % cells, 1) if shift % cells else value


SHIFTS = (0, 1, -1, GRID, -GRID)


def stencils(diffusivity):
    cell = lax.broadcasted_iota(jnp.int32, diffusivity.shape, 1)
    cells = diffusivity.shape[1]
    row, column = cell // GRID, cell % GRID
    inside = {1: column < GRID - 1, -1: column > 0, GRID: row < cells // GRID - 1, -GRID: row > 0}
    parts = {
        s: jnp.where(inside[s], 0.5 * (diffusivity + from_cell(diffusivity, s)), 0.0)
        for s in SHIFTS[1:]
    }
    parts[0] = 1.0 - (parts[1] + parts[-1] + parts[GRID] + parts[-GRID])
    return parts


def two_step_shifts():
    return sorted({a + b for a in SHIFTS for b in SHIFTS}, key=abs)


def tree_sum(terms):
    while len(terms) > 1:
        terms = [sum(terms[i + 1 : i + 2], terms[i]) for i in range(0, len(terms), 2)]
    return terms[0]


def apply_stencil(weights, shifts, value):
    return tree_sum([weights[k : k + 1] * from_cell(value, s) for k, s in enumerate(shifts)])


def tables_kernel(bands, diffusivity, gain, back, one, two, gain_high, gain_low, back_high, back_low):
    first = stencils(diffusivity[...])
    for b in range(bands):
        for k, s in enumerate(SHIFTS):
            one[b, k : k + 1, :] = first[s][b : b + 1]
    for b in range(bands):
        for c in range(bands):
            total = {}
            for s in SHIFTS:
                for r in SHIFTS:
                    term = first[s][c : c + 1] * from_cell(first[r][b : b + 1], s)
                    total[s + r] = total[s + r] + term if s + r in total else term
            for k, s in enumerate(two_step_shifts()):
                two[b * bands + c, k : k + 1, :] = total[s]
    for b in range(bands):
        gain_high[b], gain_low[b] = halves(gain[b].T)
        back_high[b], back_low[b] = halves(back[b].T)


def pairs_kernel(bands, back_high, back_low, pair_high, pair_low):
    def pair(i, carry):
        b, c = i // bands, i % bands
        high, low = back_high[b], back_low[b]
        product = dot(high, back_high[c]) + (dot(low, back_high[c]) + dot(high, back_low[c]))
        pair_high[i], pair_low[i] = halves(product)
        return carry

    lax.fori_loop(0, bands * bands, pair, 0, unroll=4)


def pack_kernel(
    bands, band_far, mask_far, observations_far, diffusivity_far, gain, back, message, band, mask, observations, diffusivity, one,
    gain_here, back_here, delta, sem,
):
    steps, records, states = observations.shape
    near = (band, mask, observations, diffusivity)
    copies = [
        pltpu.make_async_copy(a, b, sem.at[i])
        for i, (a, b) in enumerate(zip((band_far, mask_far, observations_far, diffusivity_far), near))
    ]
    for copy in copies:
        copy.start()
    for copy in copies:
        copy.wait()
    lane = lax.broadcasted_iota(jnp.int32, (META, states), 1)
    meta = jnp.zeros((META, states), F32)
    count = jnp.int32(0)
    for t in range(steps):
        seen = mask[t]
        put = lambda at, value: jnp.where(lane == at + t, value.astype(F32), meta)
        meta = put(0, band[t])
        meta = put(MASK_AT, seen)
        meta = put(SLOT_AT, count)

        @pl.when((seen > 0) & (count < SLOTS))
        def _(t=t, at=count):
            message[pl.ds(at * records, records), :] = observations[t]

        count = count + seen
    message[SLOTS * records :, :] = jnp.where(lane == COUNT_AT, count.astype(F32), meta)

    for slot in range(SLOTS):

        @pl.when(count <= slot)
        def _(slot=slot):
            message[slot * records : (slot + 1) * records, :] = jnp.zeros((records, states), F32)

    @pl.when(count > SLOTS)
    def _():
        copies = [pltpu.make_async_copy(a, b, sem.at[i]) for i, (a, b) in enumerate(((gain, gain_here), (back, back_here)))]
        for copy in copies:
            copy.start()
        first = stencils(diffusivity[...])
        for b in range(bands):
            for k, s in enumerate(SHIFTS):
                one[b, k : k + 1, :] = first[s][b : b + 1]
        for copy in copies:
            copy.wait()

        def times(rows, matrix):
            return lax.dot_general(
                rows, matrix, (((1,), (1,)), ((), ())), precision=lax.Precision.HIGHEST, preferred_element_type=F32
            )

        def forward(t, x):
            p = apply_stencil(one[band[t]], SHIFTS, x)
            delta[t] = mask[t].astype(F32) * times(observations[t] - p, gain_here[band[t]])
            return p + delta[t]

        zeros = jnp.zeros((records, states), F32)
        message[0:records, :] = lax.fori_loop(0, steps, forward, zeros)

        def backward(i, r):
            t = steps - 1 - i
            return times(r, back_here[band[t]]) + delta[t]

        message[records : 2 * records, :] = lax.fori_loop(0, steps, backward, zeros)


def main_kernel(
    bands,
    devices,
    fields,
    pieces,
    me_ref,
    band_own,
    mask_own,
    observations,
    start,
    *refs,
):
    parts, refs = refs[:pieces], refs[pieces:]
    (one, two, gain_high, gain_low, back_high, back_low, pair_high, pair_low), refs = refs[:8], refs[8:]
    filtered, smoothed, inbox, meta, table, delta, sem = refs
    steps, records, states = observations.shape
    rows = parts[0].shape[0] // (devices // pieces)
    me = me_ref[0]
    for i, part in enumerate(parts):
        each = part.shape[0]
        inbox[i * each : (i + 1) * each, :] = part[...]
    for k in range(devices):
        at = k * rows + SLOTS * records
        meta[k : k + 1, :] = inbox[at : at + 1, :].astype(jnp.int32)
    copy = pltpu.make_async_copy(meta, table, sem)
    copy.start()
    copy.wait()

    def place(block):
        apart = lax.bitwise_xor(block, me)
        found, scale = jnp.int32(0), 1
        for shift, width in reversed(fields):
            found = found + lax.bitwise_and(lax.shift_right_logical(apart, shift), width - 1) * scale
            scale *= width
        return found

    def step(b, x):
        return apply_stencil(one[b], SHIFTS, x)

    def innovation(b, difference):
        return rows_product(difference, gain_high[b], gain_low[b])

    def back(b, r):
        return rows_product(r, back_high[b], back_low[b])

    def filter_own(x):
        def body(t, x):
            b = band_own[t]
            p = step(b, x)

            def seen(p):
                change = innovation(b, observations[t] - p)
                delta[me * steps + t] = change
                return p + change

            x = lax.cond(mask_own[t] > 0, seen, lambda p: p, p)
            filtered[t] = x
            return x

        return lax.fori_loop(0, steps, body, x)

    def filter_block(block, x):
        at = place(block)
        packed = table[at, COUNT_AT] > SLOTS

        def pair(j, x):
            t = 2 * j
            b, c = table[at, t], table[at, t + 1]
            m, n = table[at, MASK_AT + t], table[at, MASK_AT + t + 1]

            def single(b, m, t, x):
                p = step(b, x)

                def seen(p):
                    row = pl.multiple_of(at * rows + lax.rem(table[at, SLOT_AT + t], SLOTS) * records, 8)
                    y = jnp.where(packed, 0.0, inbox[pl.ds(row, records), :])
                    change = innovation(b, y - p)
                    delta[block * steps + t] = change
                    return p + change

                return lax.cond(m > 0, seen, lambda p: p, p)

            return lax.cond(
                m + n > 0,
                lambda x: single(c, n, t + 1, single(b, m, t, x)),
                lambda x: apply_stencil(two[b * bands + c], two_step_shifts(), x),
                x,
            )

        x = lax.fori_loop(0, steps // 2, pair, x)
        row = pl.multiple_of(at * rows, 8)
        return lax.cond(packed, lambda x: x + inbox[pl.ds(row, records), :], lambda x: x, x)

    x = jnp.broadcast_to(start[...], (records, states))
    lax.fori_loop(
        0,
        devices,
        lambda block, x: lax.cond(block == me, filter_own, functools.partial(filter_block, block), x),
        x,
    )

    def smooth_block(i, r):
        block = devices - 1 - i
        at = place(block)

        def pair(j, r):
            t = steps - 2 - 2 * j
            b, c = table[at, t], table[at, t + 1]
            m, n = table[at, MASK_AT + t], table[at, MASK_AT + t + 1]

            def added(m, t, r):
                return lax.cond(m > 0, lambda r: r + delta[block * steps + t], lambda r: r, r)

            r = lax.cond(
                n > 0,
                lambda r: back(b, added(n, t + 1, back(c, r))),
                lambda r: rows_product(r, pair_high[c * bands + b], pair_low[c * bands + b]),
                r,
            )
            return added(m, t, r)

        r = lax.fori_loop(0, steps // 2, pair, r)
        row = pl.multiple_of(at * rows + records, 8)
        return lax.cond(table[at, COUNT_AT] > SLOTS, lambda r: r + inbox[pl.ds(row, records), :], lambda r: r, r)

    r = lax.fori_loop(0, devices - 1 - me, smooth_block, jnp.zeros((records, states), F32))

    def smooth_own(i, r):
        t = steps - 1 - i
        e = back(band_own[t], r)
        smoothed[t] = filtered[t] + e
        return lax.cond(mask_own[t] > 0, lambda e: e + delta[me * steps + t], lambda e: e, e)

    lax.fori_loop(0, steps, smooth_own, r)


def whole(memory=pltpu.VMEM):
    return pl.BlockSpec(memory_space=memory)


def xor_round(held, low, width, devices):
    return [held] + [
        lax.ppermute(held, "tm", [(i, i ^ (k << low)) for i in range(devices)]) for k in range(1, 1 << width)
    ]


def shards(observations, band_index, obs_mask, diffusivity, gain, back, initial_mean):
    steps, records, states = observations.shape
    bands = diffusivity.shape[0]
    devices = lax.axis_size("tm")
    rows = SLOTS * records + META
    params = pltpu.CompilerParams(vmem_limit_bytes=VMEM_BYTES)
    shape = jax.ShapeDtypeStruct
    message = pl.pallas_call(
        functools.partial(pack_kernel, bands),
        out_shape=shape((rows, states), F32),
        in_specs=[whole(pltpu.HBM)] * 6,
        out_specs=whole(),
        scratch_shapes=[
            pltpu.SMEM((steps,), jnp.int32),
            pltpu.SMEM((steps,), jnp.int32),
            pltpu.VMEM((steps, records, states), F32),
            pltpu.VMEM((bands, states), F32),
            pltpu.VMEM((bands, 8, states), F32),
            pltpu.VMEM((bands, states, states), F32),
            pltpu.VMEM((bands, states, states), F32),
            pltpu.VMEM((steps, records, states), F32),
            pltpu.SemaphoreType.DMA((4,)),
        ],
        compiler_params=pltpu.CompilerParams(vmem_limit_bytes=PACK_VMEM_BYTES),
        name="pack_message",
    )(band_index, obs_mask, observations, diffusivity, gain, back)
    matrix = lambda count: shape((count, states, states), BF)
    cost = lambda flops: pl.CostEstimate(flops=flops, bytes_accessed=4 * 2**20, transcendentals=0)

    def make_tables():
        return pl.pallas_call(
            functools.partial(tables_kernel, bands),
            out_shape=[shape((bands, 8, states), F32), shape((bands * bands, 16, states), F32)] + [matrix(bands)] * 4,
            in_specs=[whole()] * 3,
            out_specs=[whole()] * 6,
            compiler_params=params,
            cost_estimate=cost(2**28),
            name="tables",
        )(diffusivity, gain, back)

    def make_pairs(back_high, back_low):
        return pl.pallas_call(
            functools.partial(pairs_kernel, bands),
            out_shape=[matrix(bands * bands)] * 2,
            in_specs=[whole()] * 2,
            out_specs=[whole()] * 2,
            compiler_params=params,
            cost_estimate=cost(6 * bands**2 * states**3),
            name="pairs",
        )(back_high, back_low)

    bits = devices.bit_length() - 1
    pieces, fields, low, tables = [message], [], bits, None
    for width in [1] * (bits % 2) + [2] * (bits // 2):
        low -= width
        held = jnp.concatenate(pieces, 0)
        if fields and tables is None:
            tables = make_tables()
            held, tables = lax.optimization_barrier((held, tables))
        pieces = xor_round(held, low, width, devices)
        fields = [(low, 1 << width)] + fields
    tables = make_tables() if tables is None else tables
    tables = [*tables, *make_pairs(*tables[4:6])]
    me = lax.axis_index("tm").astype(jnp.int32)[None]
    out = shape((steps, records, states), F32)
    return pl.pallas_call(
        functools.partial(main_kernel, bands, devices, fields, len(pieces)),
        out_shape=[out, out],
        in_specs=[whole(pltpu.SMEM)] * 3 + [whole()] * (2 + len(pieces) + len(tables)),
        out_specs=[whole()] * 2,
        scratch_shapes=[
            pltpu.VMEM((devices * rows, states), F32),
            pltpu.VMEM((devices, states), jnp.int32),
            pltpu.SMEM((devices, states), jnp.int32),
            pltpu.VMEM((devices * steps, records, states), F32),
            pltpu.SemaphoreType.DMA,
        ],
        compiler_params=params,
        name="filter_and_smooth",
    )(me, band_index, obs_mask, observations, initial_mean[None, :], *pieces, *tables)


def solution(mesh):
    return jax.shard_map(
        shards,
        mesh=mesh,
        in_specs=(P("tm", "col", None), P("tm"), P("tm"), P(), P(), P(), P()),
        out_specs=(P("tm", "col", None), P("tm", "col", None)),
        check_vma=False,
    )
```

profile of v0, /device:TPU:0, one launch (start us, length us, event | category | flops | bytes accessed | tf_op | source)
XLA Modules:
  0.0 41.0 jit_solution(7680011172572460116)
XLA Ops:
  0.6 0.0 copy-start.1
  0.6 0.0 copy-start
  0.7 0.0 copy-start.3
  0.7 1.9 %pack_message.1 = f32[56,256]{1,0:T(8,128)} custom-call(s32[16]{0:T(128)} %band_own.1, s32[16]{0:T(128)} %mask_own.1, f32[16,16,256]{2,1,0:T(8,128)} %observations.1, f32[4,256]{1,0:T(4,128)} %diffusivity.1, f32[4,256,256]{2,1,0:T(8,128)} %gain.3, f32[4,256,256]{2,1,0:T(8,128)} %back.3), custom_call_target="tpu_custom_call" | custom-call | tf_op jit(solution)/shard_map/pack_message/pallas_call | solution.py:322
  2.6 0.0 copy-start.7
  2.6 4.1 %collective-permute-start = (f32[56,256]{1,0:T(8,128)}, f32[56,256]{1,0:T(8,128)S(1)}, u32[]{:S(2)}, u32[]{:S(2)}) collective-permute-start(f32[56,256]{1,0:T(8,128)} %pack_message.1), channel_id=1, source_target_pairs={{0,16},{4,20},{8,24},{12,28},{16,0},{20,4},{24,8},{28,12},{1,17},{... | collective-permute-start | bytes 172040 | tf_op jit(solution)/shard_map/ppermute | solution.py:311
  6.7 0.0 copy-done.1
  6.7 0.0 copy-done
  6.7 0.0 copy-done.3
  6.7 1.0 %tables.1 = (f32[4,8,256]{2,1,0:T(8,128)S(1)}, f32[16,16,256]{2,1,0:T(8,128)S(1)}, bf16[4,256,256]{2,1,0:T(8,128)(2,1)S(1)}, bf16[4,256,256]{2,1,0:T(8,128)(2,1)...) custom-call(f32[4,256]{1,0:T(4,128)S(1)} %copy-done.3, f32[4,256,256]{2,1,0:T(8,128)S(1)} %copy-done, ...), custom_call_target="tpu_custom_call" | custom-call | flops 268435456 | bytes 4194304 | tf_op jit(solution)/shard_map/tables/pallas_call | solution.py:345
  7.7 2.0 %collective-permute-done = f32[56,256]{1,0:T(8,128)S(1)} collective-permute-done((f32[56,256]{1,0:T(8,128)}, f32[56,256]{1,0:T(8,128)S(1)}, u32[]{:S(2)}, u32[]{:S(2)}) %collective-permute-start) | collective-permute-done | bytes 57376 | tf_op jit(solution)/shard_map/ppermute | solution.py:311
  9.7 0.0 copy-done.7
  9.7 0.0 copy-start.2
  9.7 0.0 copy-start.4
  9.7 0.0 copy-start.5
  9.7 0.0 copy-start.6
  9.7 2.4 %collective-permute-start.3 = (f32[112,256]{1,0:T(8,128)S(1)}, f32[112,256]{1,0:T(8,128)S(1)}, u32[]{:S(2)}, u32[]{:S(2)}) collective-permute-start(f32[112,256]{1,0:T(8,128)S(1)} %pad_maximum_fusion.refs_0_), channel_id=1, source_target_pairs={{0,12},{4,8},{8,4},{12,0},{16,28},{20,24},{24,20},{28,16},{1,13},{... | collective-permute-start | bytes 344072 | tf_op jit(solution)/shard_map/ppermute | solution.py:311
  12.1 0.9 %collective-permute-start.2 = (f32[112,256]{1,0:T(8,128)S(1)}, f32[112,256]{1,0:T(8,128)S(1)}, u32[]{:S(2)}, u32[]{:S(2)}) collective-permute-start(f32[112,256]{1,0:T(8,128)S(1)} %pad_maximum_fusion.refs_0_), channel_id=1, source_target_pairs={{0,8},{4,12},{8,0},{12,4},{16,24},{20,28},{24,16},{28,20},{1,9},{5... | collective-permute-start | bytes 344072 | tf_op jit(solution)/shard_map/ppermute | solution.py:311
  13.0 0.3 collective-permute-start.1
  13.3 2.3 %pairs.1 = (bf16[16,256,256]{2,1,0:T(8,128)(2,1)S(1)}, bf16[16,256,256]{2,1,0:T(8,128)(2,1)S(1)}) custom-call(bf16[4,256,256]{2,1,0:T(8,128)(2,1)S(1)} %get-tuple-element.28.back_high.refs_8_, bf16[4,256,256]{2,1,0:T(8,128)(2,1)S(1)} %get-tuple-element.29.back_low.refs_9_), custom_call_target="tpu_custom_call" | custom-call | flops 1610612736 | bytes 4194304 | tf_op jit(solution)/shard_map/pairs/pallas_call | solution.py:356
  15.6 0.0 collective-permute-done.3.refs_3_
  15.6 1.3 %collective-permute-done.2.refs_2_ = f32[112,256]{1,0:T(8,128)S(1)} collective-permute-done((f32[112,256]{1,0:T(8,128)S(1)}, f32[112,256]{1,0:T(8,128)S(1)}, u32[]{:S(2)}, u32[]{:S(2)}) %collective-permute-start.2) | collective-permute-done | bytes 114720 | tf_op jit(solution)/shard_map/ppermute | solution.py:311
  17.0 0.8 %collective-permute-done.1.refs_1_ = f32[112,256]{1,0:T(8,128)S(1)} collective-permute-done((f32[112,256]{1,0:T(8,128)S(1)}, f32[112,256]{1,0:T(8,128)S(1)}, u32[]{:S(2)}, u32[]{:S(2)}) %collective-permute-start.1) | collective-permute-done | bytes 114720 | tf_op jit(solution)/shard_map/ppermute | solution.py:311
  17.8 0.0 copy-done.2
  17.8 0.0 copy-done.4
  17.8 0.0 copy-done.5
  17.8 0.0 copy-done.6
  17.8 23.2 %filter_and_smooth.1 = (f32[16,16,256]{2,1,0:T(8,128)}, f32[16,16,256]{2,1,0:T(8,128)}) custom-call(s32[1]{0:T(128)} %bitcast.me_ref, s32[16]{0:T(128)S(1)} %copy-done.4, s32[16]{0:T(128)S(1)} %copy-done.5, f32[16,16,256]{2,1,0:T(8,128)S(1)} %copy-done.2, f32[1,256]{1,0:T(1,128)S(1)} %bitcast.2, f32[112,256]{1,0:T(8,128)S(1)} %pad_maximum_fusion.refs_0_, ...), custom_call_target="tpu_custom_call" | custom-call | tf_op jit(solution)/shard_map/filter_and_smooth/pallas_call | solution.py:380
  (1 shorter events, 0.0 us)
Async XLA Ops:
  0.6 6.1 %copy-start.1 = (f32[4,256,256]{2,1,0:T(8,128)S(1)}, f32[4,256,256]{2,1,0:T(8,128)}, u32[]{:S(2)}) copy-start(f32[4,256,256]{2,1,0:T(8,128)} %back.3) | copy-start | bytes 3145732
  0.6 6.1 %copy-start = (f32[4,256,256]{2,1,0:T(8,128)S(1)}, f32[4,256,256]{2,1,0:T(8,128)}, u32[]{:S(2)}) copy-start(f32[4,256,256]{2,1,0:T(8,128)} %gain.3) | copy-start | bytes 3145732
  0.7 6.0 %copy-start.3 = (f32[4,256]{1,0:T(4,128)S(1)}, f32[4,256]{1,0:T(4,128)}, u32[]{:S(2)}) copy-start(f32[4,256]{1,0:T(4,128)} %diffusivity.1) | copy-start | bytes 12292
  2.6 7.1 %copy-start.7 = (f32[56,256]{1,0:T(8,128)S(1)}, f32[56,256]{1,0:T(8,128)}, u32[]{:S(2)}) copy-start(f32[56,256]{1,0:T(8,128)} %pack_message.1) | copy-start | bytes 172036
  2.6 7.1 %collective-permute-start = (f32[56,256]{1,0:T(8,128)}, f32[56,256]{1,0:T(8,128)S(1)}, u32[]{:S(2)}, u32[]{:S(2)}) collective-permute-start(f32[56,256]{1,0:T(8,128)} %pack_message.1), channel_id=1, source_target_pairs={{0,16},{4,20},{8,24},{12,28},{16,0},{20,4},{24,8},{28,12},{1,17},{... | collective-permute-start | bytes 172040 | tf_op jit(solution)/shard_map/ppermute | solution.py:311
  9.7 8.1 %copy-start.2 = (f32[16,16,256]{2,1,0:T(8,128)S(1)}, f32[16,16,256]{2,1,0:T(8,128)}, u32[]{:S(2)}) copy-start(f32[16,16,256]{2,1,0:T(8,128)} %observations.1) | copy-start | bytes 786436
  9.7 8.1 %copy-start.4 = (s32[16]{0:T(128)S(1)}, s32[16]{0:T(128)}, u32[]{:S(2)}) copy-start(s32[16]{0:T(128)} %band_own.1) | copy-start | bytes 196
  9.7 8.1 %copy-start.5 = (s32[16]{0:T(128)S(1)}, s32[16]{0:T(128)}, u32[]{:S(2)}) copy-start(s32[16]{0:T(128)} %mask_own.1) | copy-start | bytes 196
  9.7 8.1 %copy-start.6 = (f32[256]{0:T(256)S(1)}, f32[256]{0:T(256)}, u32[]{:S(2)}) copy-start(f32[256]{0:T(256)} %param.13) | copy-start | bytes 3076
  9.7 5.9 %collective-permute-start.3 = (f32[112,256]{1,0:T(8,128)S(1)}, f32[112,256]{1,0:T(8,128)S(1)}, u32[]{:S(2)}, u32[]{:S(2)}) collective-permute-start(f32[112,256]{1,0:T(8,128)S(1)} %pad_maximum_fusion.refs_0_), channel_id=1, source_target_pairs={{0,12},{4,8},{8,4},{12,0},{16,28},{20,24},{24,20},{28,16},{1,13},{... | collective-permute-start | bytes 344072 | tf_op jit(solution)/shard_map/ppermute | solution.py:311
  12.1 4.9 %collective-permute-start.2 = (f32[112,256]{1,0:T(8,128)S(1)}, f32[112,256]{1,0:T(8,128)S(1)}, u32[]{:S(2)}, u32[]{:S(2)}) collective-permute-start(f32[112,256]{1,0:T(8,128)S(1)} %pad_maximum_fusion.refs_0_), channel_id=1, source_target_pairs={{0,8},{4,12},{8,0},{12,4},{16,24},{20,28},{24,16},{28,20},{1,9},{5... | collective-permute-start | bytes 344072 | tf_op jit(solution)/shard_map/ppermute | solution.py:311
  13.0 4.8 %collective-permute-start.1 = (f32[112,256]{1,0:T(8,128)S(1)}, f32[112,256]{1,0:T(8,128)S(1)}, u32[]{:S(2)}, u32[]{:S(2)}) collective-permute-start(f32[112,256]{1,0:T(8,128)S(1)} %pad_maximum_fusion.refs_0_), channel_id=1, source_target_pairs={{0,4},{4,0},{8,12},{12,8},{16,20},{20,16},{24,28},{28,24},{1,5},{5... | collective-permute-start | bytes 344072 | tf_op jit(solution)/shard_map/ppermute | solution.py:311
where the time goes:
time: 41.6 us; the launch traced here: 41 us
  Pallas kernels  28.4 us (68%)
  starting transfers between devices  7.65 us (18%)
  waiting for transfers between devices  4.13 us (10%)
  between operations  0.74 us (2%)
    pallas_call x1, Pallas kernels, shards(): pl.pallas_call(functools.partial(main_kernel, bands, devices, fields, len...  23.2 us
    ppermute x4, starting transfers between devices, xor_round(): lax.ppermute(held, 'tm', [(i, i ^ k << low) for i in range(devices)])  7.65 us
    ppermute x4, waiting for transfers between devices, xor_round(): lax.ppermute(held, 'tm', [(i, i ^ k << low) for i in range(devices)])  4.13 us
    pallas_call x1, Pallas kernels, make_pairs(): pl.pallas_call(functools.partial(pairs_kernel, bands), out_shape=[matrix(...  2.31 us
    pallas_call x1, Pallas kernels, shards(): pl.pallas_call(functools.partial(pack_kernel, bands), out_shape=shape((ro...  1.91 us
    pallas_call x1, Pallas kernels, make_tables(): pl.pallas_call(functools.partial(tables_kernel, bands), out_shape=[shape(...  0.99 us
  transfers between devices with their start and end apart: 4, of which 3 were waited for; matrix products, arithmetic and copies ran while one was open for 0% of the time, Pallas kernels for 8%

commit v1 on v0

--- a/solution.py
+++ b/solution.py
@@ -12,7 +12,8 @@
 META = 8
 MASK_AT, SLOT_AT, COUNT_AT = 32, 64, 96
 BF, F32 = jnp.bfloat16, jnp.float32
-VMEM_BYTES = 24 * 2**20
+VMEM_BYTES = 40 * 2**20
+QUADS_BYTES = 2**24
 PACK_VMEM_BYTES = 60 * 2**20
 
 
@@ -171,135 +172,195 @@
     devices,
     fields,
     pieces,
-    me_ref,
-    band_own,
-    mask_own,
     observations,
     start,
     *refs,
 ):
     parts, refs = refs[:pieces], refs[pieces:]
     (one, two, gain_high, gain_low, back_high, back_low, pair_high, pair_low), refs = refs[:8], refs[8:]
-    filtered, smoothed, inbox, meta, table, delta, sem = refs
+    (filtered_far, smoothed_far, filtered, smoothed, out_sem), refs = refs[:5], refs[5:]
+    (inbox, meta, table, delta, sem), quads = refs[:5], refs[5:]
     steps, records, states = observations.shape
     rows = parts[0].shape[0] // (devices // pieces)
-    me = me_ref[0]
-    for i, part in enumerate(parts):
-        each = part.shape[0]
-        inbox[i * each : (i + 1) * each, :] = part[...]
-    for k in range(devices):
-        at = k * rows + SLOTS * records
-        meta[k : k + 1, :] = inbox[at : at + 1, :].astype(jnp.int32)
-    copy = pltpu.make_async_copy(meta, table, sem)
-    copy.start()
-    copy.wait()
-
-    def place(block):
-        apart = lax.bitwise_xor(block, me)
+    me = lax.axis_index("tm")
+
+    def place(apart):
         found, scale = jnp.int32(0), 1
         for shift, width in reversed(fields):
             found = found + lax.bitwise_and(lax.shift_right_logical(apart, shift), width - 1) * scale
             scale *= width
         return found
 
+    def apart_at(position):
+        apart, position = 0, int(position)
+        for shift, width in reversed(fields):
+            apart |= (position % width) << shift
+            position //= width
+        return apart
+
+    each = parts[0].shape[0]
+    for k in range(devices):
+        at = k * rows + SLOTS * records - k * rows // each * each
+        block = lax.bitwise_xor(me, apart_at(k))
+        meta[pl.ds(block, 1), :] = parts[k * rows // each][at : at + 1, :].astype(jnp.int32)
+    copy = pltpu.make_async_copy(meta, table, sem)
+    copy.start()
+    for i, part in enumerate(parts):
+        inbox[i * each : (i + 1) * each, :] = part[...]
+    copy.wait()
+
     def step(b, x):
         return apply_stencil(one[b], SHIFTS, x)
 
+    def two_steps(b, c, x):
+        return apply_stencil(two[b * bands + c], two_step_shifts(), x)
+
     def innovation(b, difference):
         return rows_product(difference, gain_high[b], gain_low[b])
 
     def back(b, r):
         return rows_product(r, back_high[b], back_low[b])
 
-    def filter_own(x):
-        def body(t, x):
-            b = band_own[t]
-            p = step(b, x)
-
-            def seen(p):
-                change = innovation(b, observations[t] - p)
-                delta[me * steps + t] = change
-                return p + change
-
-            x = lax.cond(mask_own[t] > 0, seen, lambda p: p, p)
-            filtered[t] = x
+    def back_two(c, b, r):
+        return rows_product(r, pair_high[c * bands + b], pair_low[c * bands + b])
+
+    def regimes(quad):
+        block, t = quad // (steps // 4), lax.rem(quad, steps // 4) * 4
+        return block, t, [table[block, t + k] for k in range(4)], [table[block, MASK_AT + t + k] for k in range(4)]
+
+    def prepare(quad, b):
+        if quads:
+            left, right = b[3] * bands + b[2], b[1] * bands + b[0]
+            high, low = pair_high[left], pair_low[left]
+            product = dot(high, pair_high[right]) + (dot(low, pair_high[right]) + dot(high, pair_low[right]))
+            quads[0][quad], quads[1][quad] = halves(product)
+
+    def packed(block):
+        return table[block, COUNT_AT] > SLOTS
+
+    def filter_quad(quad, x):
+        block, t, b, m = regimes(quad)
+        own = block == me
+        ends = packed(block) & (t == steps - 4)
+        seen = (m[0] + m[1] + m[2] + m[3] > 0) | ends
+
+        def plain(x):
+            prepare(quad, b)
+            return two_steps(b[2], b[3], two_steps(b[0], b[1], x))
+
+        def plain_own(x):
+            prepare(quad, b)
+            filtered[t] = step(b[0], x)
+            x = two_steps(b[0], b[1], x)
+            filtered[t + 1] = x
+            filtered[t + 2] = step(b[2], x)
+            x = two_steps(b[2], b[3], x)
+            filtered[t + 3] = x
             return x
 
-        return lax.fori_loop(0, steps, body, x)
-
-    def filter_block(block, x):
-        at = place(block)
-        packed = table[at, COUNT_AT] > SLOTS
-
-        def pair(j, x):
-            t = 2 * j
-            b, c = table[at, t], table[at, t + 1]
-            m, n = table[at, MASK_AT + t], table[at, MASK_AT + t + 1]
-
-            def single(b, m, t, x):
-                p = step(b, x)
-
-                def seen(p):
-                    row = pl.multiple_of(at * rows + lax.rem(table[at, SLOT_AT + t], SLOTS) * records, 8)
-                    y = jnp.where(packed, 0.0, inbox[pl.ds(row, records), :])
-                    change = innovation(b, y - p)
-                    delta[block * steps + t] = change
-                    return p + change
-
-                return lax.cond(m > 0, seen, lambda p: p, p)
-
-            return lax.cond(
-                m + n > 0,
-                lambda x: single(c, n, t + 1, single(b, m, t, x)),
-                lambda x: apply_stencil(two[b * bands + c], two_step_shifts(), x),
-                x,
-            )
-
-        x = lax.fori_loop(0, steps // 2, pair, x)
-        row = pl.multiple_of(at * rows, 8)
-        return lax.cond(packed, lambda x: x + inbox[pl.ds(row, records), :], lambda x: x, x)
+        def observed(k, y, p):
+            change = innovation(b[k], y - p)
+            delta[quad * 4 + k] = change
+            return p + change
+
+        def seen_own(x):
+            for k in range(4):
+                p = step(b[k], x)
+                x = lax.cond(m[k] > 0, lambda p, k=k: observed(k, observations[t + k], p), lambda p: p, p)
+                filtered[t + k] = x
+            return x
+
+        def seen_other(x):
+            first = pl.multiple_of(place(lax.bitwise_xor(block, me)) * rows, 8)
+
+            def sent(k, p):
+                slot = lax.rem(table[block, SLOT_AT + t + k], SLOTS)
+                y = inbox[pl.ds(pl.multiple_of(first + slot * records, 8), records), :]
+                return observed(k, jnp.where(packed(block), 0.0, y), p)
+
+            def singles(k, x):
+                for k in (k, k + 1):
+                    x = lax.cond(m[k] > 0, lambda p, k=k: sent(k, p), lambda p: p, step(b[k], x))
+                return x
+
+            for k in (0, 2):
+                x = lax.cond(
+                    m[k] + m[k + 1] > 0, lambda x, k=k: singles(k, x), lambda x, k=k: two_steps(b[k], b[k + 1], x), x
+                )
+            return lax.cond(ends, lambda x: x + inbox[pl.ds(first, records), :], lambda x: x, x)
+
+        return lax.switch(
+            jnp.where(seen, 2, 0) + jnp.where(own, 1, 0), (plain, plain_own, seen_other, seen_own), x
+        )
 
     x = jnp.broadcast_to(start[...], (records, states))
-    lax.fori_loop(
-        0,
-        devices,
-        lambda block, x: lax.cond(block == me, filter_own, functools.partial(filter_block, block), x),
-        x,
+    per = steps // 4
+    x = lax.fori_loop(0, per * (me + 1), filter_quad, x)
+    outs = [
+        pltpu.make_async_copy(a, b, out_sem.at[i])
+        for i, (a, b) in enumerate(((filtered, filtered_far), (smoothed, smoothed_far)))
+    ]
+    outs[0].start()
+    lax.fori_loop(per * (me + 1), per * devices, filter_quad, x)
+
+    def smooth_quad(quad, r):
+        block, t, b, m = regimes(quad)
+        starts = packed(block) & (t == 0)
+        seen = (m[0] + m[1] + m[2] + m[3] > 0) | starts
+
+        def plain(r):
+            if quads:
+                return rows_product(r, quads[0][quad], quads[1][quad])
+            return back_two(b[1], b[0], back_two(b[3], b[2], r))
+
+        def added(k, r):
+            return lax.cond(m[k] > 0, lambda r: r + delta[quad * 4 + k], lambda r: r, r)
+
+        def stepped(r):
+            for k in (2, 0):
+                r = lax.cond(
+                    m[k + 1] > 0,
+                    lambda r, k=k: back(b[k], added(k + 1, back(b[k + 1], r))),
+                    lambda r, k=k: back_two(b[k + 1], b[k], r),
+                    r,
+                )
+                r = added(k, r)
+            first = place(lax.bitwise_xor(block, me)) * rows + records
+            return lax.cond(starts, lambda r: r + inbox[pl.ds(pl.multiple_of(first, 8), records), :], lambda r: r, r)
+
+        return lax.cond(seen, stepped, plain, r)
+
+    r = lax.fori_loop(
+        0, per * (devices - 1 - me), lambda i, r: smooth_quad(devices * per - 1 - i, r), jnp.zeros((records, states), F32)
     )
 
-    def smooth_block(i, r):
-        block = devices - 1 - i
-        at = place(block)
-
-        def pair(j, r):
-            t = steps - 2 - 2 * j
-            b, c = table[at, t], table[at, t + 1]
-            m, n = table[at, MASK_AT + t], table[at, MASK_AT + t + 1]
-
-            def added(m, t, r):
-                return lax.cond(m > 0, lambda r: r + delta[block * steps + t], lambda r: r, r)
-
-            r = lax.cond(
-                n > 0,
-                lambda r: back(b, added(n, t + 1, back(c, r))),
-                lambda r: rows_product(r, pair_high[c * bands + b], pair_low[c * bands + b]),
-                r,
-            )
-            return added(m, t, r)
-
-        r = lax.fori_loop(0, steps // 2, pair, r)
-        row = pl.multiple_of(at * rows + records, 8)
-        return lax.cond(table[at, COUNT_AT] > SLOTS, lambda r: r + inbox[pl.ds(row, records), :], lambda r: r, r)
-
-    r = lax.fori_loop(0, devices - 1 - me, smooth_block, jnp.zeros((records, states), F32))
-
     def smooth_own(i, r):
-        t = steps - 1 - i
-        e = back(band_own[t], r)
-        smoothed[t] = filtered[t] + e
-        return lax.cond(mask_own[t] > 0, lambda e: e + delta[me * steps + t], lambda e: e, e)
-
-    lax.fori_loop(0, steps, smooth_own, r)
+        quad = me * per + per - 1 - i
+        block, t, b, m = regimes(quad)
+        for k in (3, 2, 1, 0):
+            e = back(b[k], r)
+            smoothed[t + k] = filtered[t + k] + e
+            r = lax.cond(m[k] > 0, lambda e, k=k: e + delta[quad * 4 + k], lambda e: e, e)
+        return r
+
+    def smooth_own_plain(r):
+        own = [regimes(me * per + q) for q in range(per)]
+        after, thirds = [None] * per, [None] * per
+        for q in reversed(range(per)):
+            _, t, b, _ = own[q]
+            after[q], thirds[q] = r, back_two(b[3], b[2], r)
+            r = rows_product(r, quads[0][me * per + q], quads[1][me * per + q]) if quads else back_two(b[1], b[0], thirds[q])
+            smoothed[t] = filtered[t] + r
+        for q in reversed(range(per)):
+            _, t, b, _ = own[q]
+            for k, e in ((1, back(b[1], thirds[q])), (2, thirds[q]), (3, back(b[3], after[q]))):
+                smoothed[t + k] = filtered[t + k] + e
+        return r
+
+    lax.cond(table[me, COUNT_AT] > 0, lambda r: lax.fori_loop(0, per, smooth_own, r), smooth_own_plain, r)
+    outs[1].start()
+    for copy in outs:
+        copy.wait()
 
 
 def whole(memory=pltpu.VMEM):
@@ -375,23 +436,28 @@
         fields = [(low, 1 << width)] + fields
     tables = make_tables() if tables is None else tables
     tables = [*tables, *make_pairs(*tables[4:6])]
-    me = lax.axis_index("tm").astype(jnp.int32)[None]
     out = shape((steps, records, states), F32)
+    quads = devices * steps // 4
+    deep = quads * states * states * 4 <= QUADS_BYTES
     return pl.pallas_call(
         functools.partial(main_kernel, bands, devices, fields, len(pieces)),
         out_shape=[out, out],
-        in_specs=[whole(pltpu.SMEM)] * 3 + [whole()] * (2 + len(pieces) + len(tables)),
-        out_specs=[whole()] * 2,
+        in_specs=[whole()] * (2 + len(pieces) + len(tables)),
+        out_specs=[whole(pltpu.HBM)] * 2,
         scratch_shapes=[
+            pltpu.VMEM((steps, records, states), F32),
+            pltpu.VMEM((steps, records, states), F32),
+            pltpu.SemaphoreType.DMA((2,)),
             pltpu.VMEM((devices * rows, states), F32),
             pltpu.VMEM((devices, states), jnp.int32),
             pltpu.SMEM((devices, states), jnp.int32),
             pltpu.VMEM((devices * steps, records, states), F32),
             pltpu.SemaphoreType.DMA,
-        ],
+        ]
+        + [pltpu.VMEM((quads, states, states), BF)] * (2 * deep),
         compiler_params=params,
         name="filter_and_smooth",
-    )(me, band_index, obs_mask, observations, initial_mean[None, :], *pieces, *tables)
+    )(observations, initial_mean[None, :], *pieces, *tables)
 
 
 def solution(mesh):

time: 41.6 us -> 39.8 us (0.957)
  Pallas kernels: 28.4 us -> 26.9 us
    pallas_call x1, Pallas kernels: 23.2 us -> 21.7 us  [shards(): pl.pallas_call(functools.partial(main_kernel, bands, devices, fields, len...]
where the time goes in v1:
time: 39.8 us; the launch traced here: 39.4 us
  Pallas kernels  26.9 us (68%)
  starting transfers between devices  7.65 us (19%)
  waiting for transfers between devices  4.13 us (10%)
  between operations  0.71 us (2%)
    pallas_call x1, Pallas kernels, shards(): pl.pallas_call(functools.partial(main_kernel, bands, devices, fields, len...  21.7 us
    ppermute x4, starting transfers between devices, xor_round(): lax.ppermute(held, 'tm', [(i, i ^ k << low) for i in range(devices)])  7.65 us
    ppermute x4, waiting for transfers between devices, xor_round(): lax.ppermute(held, 'tm', [(i, i ^ k << low) for i in range(devices)])  4.13 us
    pallas_call x1, Pallas kernels, make_pairs(): pl.pallas_call(functools.partial(pairs_kernel, bands), out_shape=[matrix(...  2.31 us
    pallas_call x1, Pallas kernels, shards(): pl.pallas_call(functools.partial(pack_kernel, bands), out_shape=shape((ro...  1.91 us
    pallas_call x1, Pallas kernels, make_tables(): pl.pallas_call(functools.partial(tables_kernel, bands), out_shape=[shape(...  0.99 us
  transfers between devices with their start and end apart: 4, of which 3 were waited for; matrix products, arithmetic and copies ran while one was open for 0% of the time, Pallas kernels for 8%

profile of v1, /device:TPU:0, one launch (start us, length us, event | category | flops | bytes accessed | tf_op | source)
XLA Modules:
  0.0 39.4 jit_solution(13622035991973201283)
XLA Ops:
  0.6 0.0 copy-start.1
  0.6 0.0 copy-start
  0.7 0.0 copy-start.3
  0.7 1.9 %pack_message.1 = f32[56,256]{1,0:T(8,128)} custom-call(s32[16]{0:T(128)} %band_far.1, s32[16]{0:T(128)} %mask_far.1, f32[16,16,256]{2,1,0:T(8,128)} %observations.1, f32[4,256]{1,0:T(4,128)} %diffusivity.1, f32[4,256,256]{2,1,0:T(8,128)} %gain.3, f32[4,256,256]{2,1,0:T(8,128)} %back.3), custom_call_target="tpu_custom_call" | custom-call | tf_op jit(solution)/shard_map/pack_message/pallas_call | solution.py:383
  2.6 0.0 copy-start.5
  2.6 4.1 %collective-permute-start = (f32[56,256]{1,0:T(8,128)}, f32[56,256]{1,0:T(8,128)S(1)}, u32[]{:S(2)}, u32[]{:S(2)}) collective-permute-start(f32[56,256]{1,0:T(8,128)} %pack_message.1), channel_id=1, source_target_pairs={{0,16},{4,20},{8,24},{12,28},{16,0},{20,4},{24,8},{28,12},{1,17},{... | collective-permute-start | bytes 172040 | tf_op jit(solution)/shard_map/ppermute | solution.py:372
  6.7 0.0 copy-done.1
  6.7 0.0 copy-done
  6.7 0.0 copy-done.3
  6.7 1.0 %tables.1 = (f32[4,8,256]{2,1,0:T(8,128)S(1)}, f32[16,16,256]{2,1,0:T(8,128)S(1)}, bf16[4,256,256]{2,1,0:T(8,128)(2,1)S(1)}, bf16[4,256,256]{2,1,0:T(8,128)(2,1)...) custom-call(f32[4,256]{1,0:T(4,128)S(1)} %copy-done.3, f32[4,256,256]{2,1,0:T(8,128)S(1)} %copy-done, ...), custom_call_target="tpu_custom_call" | custom-call | flops 268435456 | bytes 4194304 | tf_op jit(solution)/shard_map/tables/pallas_call | solution.py:406
  7.7 2.0 %collective-permute-done = f32[56,256]{1,0:T(8,128)S(1)} collective-permute-done((f32[56,256]{1,0:T(8,128)}, f32[56,256]{1,0:T(8,128)S(1)}, u32[]{:S(2)}, u32[]{:S(2)}) %collective-permute-start) | collective-permute-done | bytes 57376 | tf_op jit(solution)/shard_map/ppermute | solution.py:372
  9.7 0.0 copy-done.5
  9.7 0.0 copy-start.2
  9.7 0.0 copy-start.4
  9.7 2.4 %collective-permute-start.3 = (f32[112,256]{1,0:T(8,128)S(1)}, f32[112,256]{1,0:T(8,128)S(1)}, u32[]{:S(2)}, u32[]{:S(2)}) collective-permute-start(f32[112,256]{1,0:T(8,128)S(1)} %pad_maximum_fusion.refs_0_), channel_id=1, source_target_pairs={{0,12},{4,8},{8,4},{12,0},{16,28},{20,24},{24,20},{28,16},{1,13},{... | collective-permute-start | bytes 344072 | tf_op jit(solution)/shard_map/ppermute | solution.py:372
  12.1 0.9 %collective-permute-start.2 = (f32[112,256]{1,0:T(8,128)S(1)}, f32[112,256]{1,0:T(8,128)S(1)}, u32[]{:S(2)}, u32[]{:S(2)}) collective-permute-start(f32[112,256]{1,0:T(8,128)S(1)} %pad_maximum_fusion.refs_0_), channel_id=1, source_target_pairs={{0,8},{4,12},{8,0},{12,4},{16,24},{20,28},{24,16},{28,20},{1,9},{5... | collective-permute-start | bytes 344072 | tf_op jit(solution)/shard_map/ppermute | solution.py:372
  12.9 0.3 collective-permute-start.1
  13.3 2.3 %pairs.1 = (bf16[16,256,256]{2,1,0:T(8,128)(2,1)S(1)}, bf16[16,256,256]{2,1,0:T(8,128)(2,1)S(1)}) custom-call(bf16[4,256,256]{2,1,0:T(8,128)(2,1)S(1)} %get-tuple-element.28.back_high.refs_8_, bf16[4,256,256]{2,1,0:T(8,128)(2,1)S(1)} %get-tuple-element.29.back_low.refs_9_), custom_call_target="tpu_custom_call" | custom-call | flops 1610612736 | bytes 4194304 | tf_op jit(solution)/shard_map/pairs/pallas_call | solution.py:417
  15.6 0.0 collective-permute-done.3.refs_3_
  15.6 1.3 %collective-permute-done.2.refs_2_ = f32[112,256]{1,0:T(8,128)S(1)} collective-permute-done((f32[112,256]{1,0:T(8,128)S(1)}, f32[112,256]{1,0:T(8,128)S(1)}, u32[]{:S(2)}, u32[]{:S(2)}) %collective-permute-start.2) | collective-permute-done | bytes 114720 | tf_op jit(solution)/shard_map/ppermute | solution.py:372
  16.9 0.8 %collective-permute-done.1.refs_1_ = f32[112,256]{1,0:T(8,128)S(1)} collective-permute-done((f32[112,256]{1,0:T(8,128)S(1)}, f32[112,256]{1,0:T(8,128)S(1)}, u32[]{:S(2)}, u32[]{:S(2)}) %collective-permute-start.1) | collective-permute-done | bytes 114720 | tf_op jit(solution)/shard_map/ppermute | solution.py:372
  17.7 0.0 copy-done.2
  17.7 0.0 copy-done.4
  17.7 21.7 %filter_and_smooth.1 = (f32[16,16,256]{2,1,0:T(8,128)}, f32[16,16,256]{2,1,0:T(8,128)}) custom-call(f32[16,16,256]{2,1,0:T(8,128)S(1)} %copy-done.2, f32[1,256]{1,0:T(1,128)S(1)} %bitcast.1, f32[112,256]{1,0:T(8,128)S(1)} %pad_maximum_fusion.refs_0_, f32[112,256]{1,0:T(8,128)S(1)} %collective-permute-done.1.refs_1_, ...), custom_call_target="tpu_custom_call" | custom-call | tf_op jit(solution)/shard_map/filter_and_smooth/pallas_call | solution.py:442
  (1 shorter events, 0.0 us)
Async XLA Ops:
  0.6 6.1 %copy-start.1 = (f32[4,256,256]{2,1,0:T(8,128)S(1)}, f32[4,256,256]{2,1,0:T(8,128)}, u32[]{:S(2)}) copy-start(f32[4,256,256]{2,1,0:T(8,128)} %back.3) | copy-start | bytes 3145732
  0.6 6.0 %copy-start = (f32[4,256,256]{2,1,0:T(8,128)S(1)}, f32[4,256,256]{2,1,0:T(8,128)}, u32[]{:S(2)}) copy-start(f32[4,256,256]{2,1,0:T(8,128)} %gain.3) | copy-start | bytes 3145732
  0.7 6.0 %copy-start.3 = (f32[4,256]{1,0:T(4,128)S(1)}, f32[4,256]{1,0:T(4,128)}, u32[]{:S(2)}) copy-start(f32[4,256]{1,0:T(4,128)} %diffusivity.1) | copy-start | bytes 12292
  2.6 7.1 %copy-start.5 = (f32[56,256]{1,0:T(8,128)S(1)}, f32[56,256]{1,0:T(8,128)}, u32[]{:S(2)}) copy-start(f32[56,256]{1,0:T(8,128)} %pack_message.1) | copy-start | bytes 172036
  2.6 7.1 %collective-permute-start = (f32[56,256]{1,0:T(8,128)}, f32[56,256]{1,0:T(8,128)S(1)}, u32[]{:S(2)}, u32[]{:S(2)}) collective-permute-start(f32[56,256]{1,0:T(8,128)} %pack_message.1), channel_id=1, source_target_pairs={{0,16},{4,20},{8,24},{12,28},{16,0},{20,4},{24,8},{28,12},{1,17},{... | collective-permute-start | bytes 172040 | tf_op jit(solution)/shard_map/ppermute | solution.py:372
  9.7 8.1 %copy-start.2 = (f32[16,16,256]{2,1,0:T(8,128)S(1)}, f32[16,16,256]{2,1,0:T(8,128)}, u32[]{:S(2)}) copy-start(f32[16,16,256]{2,1,0:T(8,128)} %observations.1) | copy-start | bytes 786436
  9.7 8.0 %copy-start.4 = (f32[256]{0:T(256)S(1)}, f32[256]{0:T(256)}, u32[]{:S(2)}) copy-start(f32[256]{0:T(256)} %param.13) | copy-start | bytes 3076
  9.7 5.9 %collective-permute-start.3 = (f32[112,256]{1,0:T(8,128)S(1)}, f32[112,256]{1,0:T(8,128)S(1)}, u32[]{:S(2)}, u32[]{:S(2)}) collective-permute-start(f32[112,256]{1,0:T(8,128)S(1)} %pad_maximum_fusion.refs_0_), channel_id=1, source_target_pairs={{0,12},{4,8},{8,4},{12,0},{16,28},{20,24},{24,20},{28,16},{1,13},{... | collective-permute-start | bytes 344072 | tf_op jit(solution)/shard_map/ppermute | solution.py:372
  12.1 4.9 %collective-permute-start.2 = (f32[112,256]{1,0:T(8,128)S(1)}, f32[112,256]{1,0:T(8,128)S(1)}, u32[]{:S(2)}, u32[]{:S(2)}) collective-permute-start(f32[112,256]{1,0:T(8,128)S(1)} %pad_maximum_fusion.refs_0_), channel_id=1, source_target_pairs={{0,8},{4,12},{8,0},{12,4},{16,24},{20,28},{24,16},{28,20},{1,9},{5... | collective-permute-start | bytes 344072 | tf_op jit(solution)/shard_map/ppermute | solution.py:372
  12.9 4.8 %collective-permute-start.1 = (f32[112,256]{1,0:T(8,128)S(1)}, f32[112,256]{1,0:T(8,128)S(1)}, u32[]{:S(2)}, u32[]{:S(2)}) collective-permute-start(f32[112,256]{1,0:T(8,128)S(1)} %pad_maximum_fusion.refs_0_), channel_id=1, source_target_pairs={{0,4},{4,0},{8,12},{12,8},{16,20},{20,16},{24,28},{28,24},{1,5},{5... | collective-permute-start | bytes 344072 | tf_op jit(solution)/shard_map/ppermute | solution.py:372

commit v2 on v1

--- a/solution.py
+++ b/solution.py
@@ -10,11 +10,18 @@
 GRID = 16
 SLOTS = 3
 META = 8
-MASK_AT, SLOT_AT, COUNT_AT = 32, 64, 96
 BF, F32 = jnp.bfloat16, jnp.float32
 VMEM_BYTES = 40 * 2**20
 QUADS_BYTES = 2**24
 PACK_VMEM_BYTES = 60 * 2**20
+
+
+def lanes(steps):
+    at, places = 0, []
+    for size in (steps, steps, steps, steps // 2, steps // 4, steps // 4, steps // 8, steps // 8, 1):
+        places.append(at)
+        at += size
+    return places
 
 
 def halves(value):
@@ -89,9 +96,9 @@
 
 def pairs_kernel(bands, back_high, back_low, pair_high, pair_low):
     def pair(i, carry):
-        b, c = i // bands, i % bands
-        high, low = back_high[b], back_low[b]
-        product = dot(high, back_high[c]) + (dot(low, back_high[c]) + dot(high, back_low[c]))
+        earlier, later = i // bands, i % bands
+        high, low = back_high[later], back_low[later]
+        product = dot(high, back_high[earlier]) + (dot(low, back_high[earlier]) + dot(high, back_low[earlier]))
         pair_high[i], pair_low[i] = halves(product)
         return carry
 
@@ -113,21 +120,40 @@
     for copy in copies:
         copy.wait()
     lane = lax.broadcasted_iota(jnp.int32, (META, states), 1)
-    meta = jnp.zeros((META, states), F32)
+    meta = jnp.zeros((META, states), jnp.int32)
+    band_at, mask_at, slot_at, pair_at, quad_at, quad_own_at, oct_at, oct_own_at, count_at = lanes(steps)
+
+    def put(at, value):
+        return jnp.where(lane == at, value, meta)
+
     count = jnp.int32(0)
     for t in range(steps):
-        seen = mask[t]
-        put = lambda at, value: jnp.where(lane == at + t, value.astype(F32), meta)
-        meta = put(0, band[t])
-        meta = put(MASK_AT, seen)
-        meta = put(SLOT_AT, count)
-
-        @pl.when((seen > 0) & (count < SLOTS))
+        meta = put(band_at + t, band[t])
+        meta = put(mask_at + t, mask[t])
+        meta = put(slot_at + t, count)
+
+        @pl.when((mask[t] > 0) & (count < SLOTS))
         def _(t=t, at=count):
             message[pl.ds(at * records, records), :] = observations[t]
 
-        count = count + seen
-    message[SLOTS * records :, :] = jnp.where(lane == COUNT_AT, count.astype(F32), meta)
+        count = count + mask[t]
+    packed = count > SLOTS
+    for p in range(steps // 2):
+        meta = put(pair_at + p, band[2 * p] * bands + band[2 * p + 1])
+    ways, ways_own = [], []
+    for q in range(steps // 4):
+        m = [mask[4 * q + k] for k in range(4)]
+        seen = m[0] + m[1] + m[2] + m[3]
+        way = jnp.where(seen == 1, 2 + m[1] + 2 * m[2] + 3 * m[3], jnp.where(seen > 1, 1, 0))
+        ways_own.append(way)
+        ways.append(jnp.where(packed & ((seen > 0) | (q in (0, steps // 4 - 1))), 1, way))
+        meta = put(quad_at + q, ways[q])
+        meta = put(quad_own_at + q, way)
+    for o in range(steps // 8):
+        meta = put(oct_at + o, ways[2 * o] + ways[2 * o + 1])
+        meta = put(oct_own_at + o, ways_own[2 * o] + ways_own[2 * o + 1])
+    meta = put(count_at, count)
+    message[SLOTS * records :, :] = meta.astype(F32)
 
     for slot in range(SLOTS):
 
@@ -135,7 +161,7 @@
         def _(slot=slot):
             message[slot * records : (slot + 1) * records, :] = jnp.zeros((records, states), F32)
 
-    @pl.when(count > SLOTS)
+    @pl.when(packed)
     def _():
         copies = [pltpu.make_async_copy(a, b, sem.at[i]) for i, (a, b) in enumerate(((gain, gain_here), (back, back_here)))]
         for copy in copies:
@@ -178,9 +204,10 @@
 ):
     parts, refs = refs[:pieces], refs[pieces:]
     (one, two, gain_high, gain_low, back_high, back_low, pair_high, pair_low), refs = refs[:8], refs[8:]
-    (filtered_far, smoothed_far, filtered, smoothed, out_sem), refs = refs[:5], refs[5:]
-    (inbox, meta, table, delta, sem), quads = refs[:5], refs[5:]
+    (filtered_far, smoothed_far, held, smoothed, out_sem), refs = refs[:5], refs[5:]
+    (inbox, meta, table, delta, pushed, sem), quads = refs[:6], refs[6:]
     steps, records, states = observations.shape
+    per = steps // 4
     rows = parts[0].shape[0] // (devices // pieces)
     me = lax.axis_index("tm")
 
@@ -212,8 +239,8 @@
     def step(b, x):
         return apply_stencil(one[b], SHIFTS, x)
 
-    def two_steps(b, c, x):
-        return apply_stencil(two[b * bands + c], two_step_shifts(), x)
+    def two_steps(pair, x):
+        return apply_stencil(two[pair], two_step_shifts(), x)
 
     def innovation(b, difference):
         return rows_product(difference, gain_high[b], gain_low[b])
@@ -221,143 +248,152 @@
     def back(b, r):
         return rows_product(r, back_high[b], back_low[b])
 
-    def back_two(c, b, r):
-        return rows_product(r, pair_high[c * bands + b], pair_low[c * bands + b])
-
-    def regimes(quad):
-        block, t = quad // (steps // 4), lax.rem(quad, steps // 4) * 4
-        return block, t, [table[block, t + k] for k in range(4)], [table[block, MASK_AT + t + k] for k in range(4)]
-
-    def prepare(quad, b):
+    def back_two(pair, r):
+        return rows_product(r, pair_high[pair], pair_low[pair])
+
+    band_at, mask_at, slot_at, pair_at, quad_at, quad_own_at, oct_at, oct_own_at, count_at = lanes(steps)
+
+    def pairs(block, q):
+        return table[block, pair_at + 2 * q], table[block, pair_at + 2 * q + 1]
+
+    def four(at, block, q):
+        return [table[block, at + 4 * q + k] for k in range(4)]
+
+    def prepare(block, q):
         if quads:
-            left, right = b[3] * bands + b[2], b[1] * bands + b[0]
+            right, left = pairs(block, q)
             high, low = pair_high[left], pair_low[left]
             product = dot(high, pair_high[right]) + (dot(low, pair_high[right]) + dot(high, pair_low[right]))
-            quads[0][quad], quads[1][quad] = halves(product)
-
-    def packed(block):
-        return table[block, COUNT_AT] > SLOTS
-
-    def filter_quad(quad, x):
-        block, t, b, m = regimes(quad)
+            quads[0][block * per + q], quads[1][block * per + q] = halves(product)
+
+    def over_quad(block, q, r):
+        if quads:
+            return rows_product(r, quads[0][block * per + q], quads[1][block * per + q])
+        early, late = pairs(block, q)
+        return back_two(early, back_two(late, r))
+
+    def added(seen, at, r):
+        return jnp.where(seen > 0, r + delta[at], r)
+
+    def plain(block, q, x):
+        early, late = pairs(block, q)
+        at = (block * per + q) * 4 + 1
+        prepare(block, q)
+        pushed[block * per + q] = jnp.zeros_like(x)
+        x = two_steps(early, x)
+        held[at + 1] = x
+        x = two_steps(late, x)
+        held[at + 3] = x
+        return x
+
+    def filter_quad(block, q, x):
+        at = (block * per + q) * 4
         own = block == me
-        ends = packed(block) & (t == steps - 4)
-        seen = (m[0] + m[1] + m[2] + m[3] > 0) | ends
-
-        def plain(x):
-            prepare(quad, b)
-            return two_steps(b[2], b[3], two_steps(b[0], b[1], x))
-
-        def plain_own(x):
-            prepare(quad, b)
-            filtered[t] = step(b[0], x)
-            x = two_steps(b[0], b[1], x)
-            filtered[t + 1] = x
-            filtered[t + 2] = step(b[2], x)
-            x = two_steps(b[2], b[3], x)
-            filtered[t + 3] = x
+        first = pl.multiple_of(place(lax.bitwise_xor(block, me)) * rows, 8)
+
+        def keep(k, x):
+            held[at + k + 1] = x
             return x
 
-        def observed(k, y, p):
-            change = innovation(b[k], y - p)
-            delta[quad * 4 + k] = change
-            return p + change
-
-        def seen_own(x):
+        def corrected(b, k, p, packed=False):
+            slot = lax.rem(table[block, slot_at + 4 * q + k], SLOTS)
+            sent = inbox[pl.ds(pl.multiple_of(first + slot * records, 8), records), :]
+            y = jnp.where(packed, 0.0, jnp.where(own, observations[4 * q + k], sent))
+            change = innovation(b, y - p)
+            delta[at + k] = change
+            return change
+
+        def one_seen(k, x):
+            b = four(band_at, block, q)
+            early, late = pairs(block, q)
+            prepare(block, q)
+            if k >= 2:
+                x = keep(1, two_steps(early, x))
+            if k % 2:
+                x = keep(k - 1, step(b[k - 1], x))
+            p = step(b[k], x)
+            change = corrected(b[k], k, p)
+            x = keep(k, p + change)
+            if k % 2 == 0:
+                x = keep(k + 1, step(b[k + 1], x))
+            if k < 2:
+                x = keep(3, two_steps(late, x))
+            if k == 0:
+                change = jnp.zeros_like(x)
+            elif k == 1:
+                change = back(b[0], change)
+            else:
+                change = back_two(early, change if k == 2 else back(b[2], change))
+            pushed[block * per + q] = change
+            return x
+
+        def any_seen(x):
+            b, m = four(band_at, block, q), four(mask_at, block, q)
+            packed = (table[block, count_at] > SLOTS) & jnp.logical_not(own)
+            prepare(block, q)
             for k in range(4):
                 p = step(b[k], x)
-                x = lax.cond(m[k] > 0, lambda p, k=k: observed(k, observations[t + k], p), lambda p: p, p)
-                filtered[t + k] = x
-            return x
-
-        def seen_other(x):
-            first = pl.multiple_of(place(lax.bitwise_xor(block, me)) * rows, 8)
-
-            def sent(k, p):
-                slot = lax.rem(table[block, SLOT_AT + t + k], SLOTS)
-                y = inbox[pl.ds(pl.multiple_of(first + slot * records, 8), records), :]
-                return observed(k, jnp.where(packed(block), 0.0, y), p)
-
-            def singles(k, x):
-                for k in (k, k + 1):
-                    x = lax.cond(m[k] > 0, lambda p, k=k: sent(k, p), lambda p: p, step(b[k], x))
-                return x
-
-            for k in (0, 2):
-                x = lax.cond(
-                    m[k] + m[k + 1] > 0, lambda x, k=k: singles(k, x), lambda x, k=k: two_steps(b[k], b[k + 1], x), x
-                )
-            return lax.cond(ends, lambda x: x + inbox[pl.ds(first, records), :], lambda x: x, x)
+                x = keep(k, lax.cond(m[k] > 0, lambda p, k=k: p + corrected(b[k], k, p, packed), lambda p: p, p))
+            r = jnp.zeros_like(x)
+            for k in (3, 2, 1):
+                r = back(b[k - 1], added(m[k], at + k, r))
+            r_sent = inbox[pl.ds(pl.multiple_of(first + records, 8), records), :]
+            pushed[block * per + q] = jnp.where(packed & (q == 0), r + r_sent, r)
+            return keep(3, jnp.where(packed & (q == per - 1), x + inbox[pl.ds(first, records), :], x))
 
         return lax.switch(
-            jnp.where(seen, 2, 0) + jnp.where(own, 1, 0), (plain, plain_own, seen_other, seen_own), x
+            table[block, jnp.where(own, quad_own_at, quad_at) + q],
+            [functools.partial(plain, block, q), any_seen] + [functools.partial(one_seen, k) for k in range(4)],
+            x,
         )
 
-    x = jnp.broadcast_to(start[...], (records, states))
-    per = steps // 4
-    x = lax.fori_loop(0, per * (me + 1), filter_quad, x)
+    def filter_oct(block, o, x):
+        return lax.cond(
+            table[block, jnp.where(block == me, oct_own_at, oct_at) + o] == 0,
+            lambda x: plain(block, 2 * o + 1, plain(block, 2 * o, x)),
+            lambda x: lax.fori_loop(2 * o, 2 * o + 2, functools.partial(filter_quad, block), x),
+            x,
+        )
+
+    def filter_block(block, x):
+        return lax.fori_loop(0, per // 2, functools.partial(filter_oct, block), x)
+
+    held[0] = jnp.broadcast_to(start[...], (records, states))
+    x = lax.fori_loop(0, me + 1, filter_block, held[0])
+    own_bands = [four(band_at, me, q) for q in range(per)]
+    own_masks = [four(mask_at, me, q) for q in range(per)]
+    for q in range(per):
+        for k in (0, 2):
+            at = me * steps + q * 4 + k
+            seen = own_masks[q][k] + own_masks[q][k + 1] > 0
+            held[at + 1] = jnp.where(seen, held[at + 1], step(own_bands[q][k], held[at]))
     outs = [
         pltpu.make_async_copy(a, b, out_sem.at[i])
-        for i, (a, b) in enumerate(((filtered, filtered_far), (smoothed, smoothed_far)))
+        for i, (a, b) in enumerate(((held.at[pl.ds(me * steps + 1, steps)], filtered_far), (smoothed, smoothed_far)))
     ]
     outs[0].start()
-    lax.fori_loop(per * (me + 1), per * devices, filter_quad, x)
-
-    def smooth_quad(quad, r):
-        block, t, b, m = regimes(quad)
-        starts = packed(block) & (t == 0)
-        seen = (m[0] + m[1] + m[2] + m[3] > 0) | starts
-
-        def plain(r):
-            if quads:
-                return rows_product(r, quads[0][quad], quads[1][quad])
-            return back_two(b[1], b[0], back_two(b[3], b[2], r))
-
-        def added(k, r):
-            return lax.cond(m[k] > 0, lambda r: r + delta[quad * 4 + k], lambda r: r, r)
-
-        def stepped(r):
-            for k in (2, 0):
-                r = lax.cond(
-                    m[k + 1] > 0,
-                    lambda r, k=k: back(b[k], added(k + 1, back(b[k + 1], r))),
-                    lambda r, k=k: back_two(b[k + 1], b[k], r),
-                    r,
-                )
-                r = added(k, r)
-            first = place(lax.bitwise_xor(block, me)) * rows + records
-            return lax.cond(starts, lambda r: r + inbox[pl.ds(pl.multiple_of(first, 8), records), :], lambda r: r, r)
-
-        return lax.cond(seen, stepped, plain, r)
-
-    r = lax.fori_loop(
-        0, per * (devices - 1 - me), lambda i, r: smooth_quad(devices * per - 1 - i, r), jnp.zeros((records, states), F32)
-    )
-
-    def smooth_own(i, r):
-        quad = me * per + per - 1 - i
-        block, t, b, m = regimes(quad)
-        for k in (3, 2, 1, 0):
-            e = back(b[k], r)
-            smoothed[t + k] = filtered[t + k] + e
-            r = lax.cond(m[k] > 0, lambda e, k=k: e + delta[quad * 4 + k], lambda e: e, e)
+    lax.fori_loop(me + 1, devices, filter_block, x)
+
+    def smooth_block(i, r):
+        block = devices - 1 - i
+        for q in reversed(range(per)):
+            r = over_quad(block, q, r) + pushed[block * per + q]
+            r = added(table[block, mask_at + 4 * q], block * steps + 4 * q, r)
         return r
 
-    def smooth_own_plain(r):
-        own = [regimes(me * per + q) for q in range(per)]
-        after, thirds = [None] * per, [None] * per
-        for q in reversed(range(per)):
-            _, t, b, _ = own[q]
-            after[q], thirds[q] = r, back_two(b[3], b[2], r)
-            r = rows_product(r, quads[0][me * per + q], quads[1][me * per + q]) if quads else back_two(b[1], b[0], thirds[q])
-            smoothed[t] = filtered[t] + r
-        for q in reversed(range(per)):
-            _, t, b, _ = own[q]
-            for k, e in ((1, back(b[1], thirds[q])), (2, thirds[q]), (3, back(b[3], after[q]))):
-                smoothed[t + k] = filtered[t + k] + e
-        return r
-
-    lax.cond(table[me, COUNT_AT] > 0, lambda r: lax.fori_loop(0, per, smooth_own, r), smooth_own_plain, r)
+    r = lax.fori_loop(0, devices - 1 - me, smooth_block, jnp.zeros((records, states), F32))
+
+    def smooth(q, k, e):
+        smoothed[q * 4 + k] = held[me * steps + q * 4 + k + 1] + e
+        return added(own_masks[q][k], me * steps + q * 4 + k, e)
+
+    after = [None] * per
+    for q in reversed(range(per)):
+        after[q] = r
+        r = smooth(q, 0, over_quad(me, q, r) + pushed[me * per + q])
+    for k in (3, 2, 1):
+        for q in range(per):
+            after[q] = smooth(q, k, back(own_bands[q][k], after[q]))
     outs[1].start()
     for copy in outs:
         copy.wait()
@@ -445,13 +481,14 @@
         in_specs=[whole()] * (2 + len(pieces) + len(tables)),
         out_specs=[whole(pltpu.HBM)] * 2,
         scratch_shapes=[
-            pltpu.VMEM((steps, records, states), F32),
+            pltpu.VMEM((devices * steps + 1, records, states), F32),
             pltpu.VMEM((steps, records, states), F32),
             pltpu.SemaphoreType.DMA((2,)),
             pltpu.VMEM((devices * rows, states), F32),
             pltpu.VMEM((devices, states), jnp.int32),
             pltpu.SMEM((devices, states), jnp.int32),
             pltpu.VMEM((devices * steps, records, states), F32),
+            pltpu.VMEM((quads, records, states), F32),
             pltpu.SemaphoreType.DMA,
         ]
         + [pltpu.VMEM((quads, states, states), BF)] * (2 * deep),

time: 39.8 us -> 36.2 us (0.910)
  Pallas kernels: 26.9 us -> 23.3 us
    pallas_call x1, Pallas kernels: 21.7 us -> 18 us  [shards(): pl.pallas_call(functools.partial(main_kernel, bands, devices, fields, len...]
  transfers between devices with their start and end apart: 4 -> 4, of which waited for: 3 -> 3; matrix products, arithmetic and copies ran while one was open for 0% -> 0% of each run, Pallas kernels for 8% -> 9%
where the time goes in v2:
time: 36.2 us; the launch traced here: 35.8 us
  Pallas kernels  23.3 us (64%)
  starting transfers between devices  7.65 us (21%)
  waiting for transfers between devices  4.09 us (11%)
  between operations  0.72 us (2%)
    pallas_call x1, Pallas kernels, shards(): pl.pallas_call(functools.partial(main_kernel, bands, devices, fields, len...  18 us
    ppermute x4, starting transfers between devices, xor_round(): lax.ppermute(held, 'tm', [(i, i ^ k << low) for i in range(devices)])  7.65 us
    ppermute x4, waiting for transfers between devices, xor_round(): lax.ppermute(held, 'tm', [(i, i ^ k << low) for i in range(devices)])  4.09 us
    pallas_call x1, Pallas kernels, make_pairs(): pl.pallas_call(functools.partial(pairs_kernel, bands), out_shape=[matrix(...  2.35 us
    pallas_call x1, Pallas kernels, shards(): pl.pallas_call(functools.partial(pack_kernel, bands), out_shape=shape((ro...  1.94 us
    pallas_call x1, Pallas kernels, make_tables(): pl.pallas_call(functools.partial(tables_kernel, bands), out_shape=[shape(...  0.99 us
  transfers between devices with their start and end apart: 4, of which 3 were waited for; matrix products, arithmetic and copies ran while one was open for 0% of the time, Pallas kernels for 9%

profile of v2, /device:TPU:0, one launch (start us, length us, event | category | flops | bytes accessed | tf_op | source)
XLA Modules:
  0.0 35.8 jit_solution(5318576309058455171)
XLA Ops:
  0.6 0.0 copy-start.1
  0.6 0.0 copy-start
  0.7 0.0 copy-start.3
  0.7 1.9 %pack_message.1 = f32[56,256]{1,0:T(8,128)} custom-call(s32[16]{0:T(128)} %band_far.1, s32[16]{0:T(128)} %mask_far.1, f32[16,16,256]{2,1,0:T(8,128)} %observations.1, f32[4,256]{1,0:T(4,128)} %diffusivity.1, f32[4,256,256]{2,1,0:T(8,128)} %gain.3, f32[4,256,256]{2,1,0:T(8,128)} %back.3), custom_call_target="tpu_custom_call" | custom-call | tf_op jit(solution)/shard_map/pack_message/pallas_call | solution.py:419
  2.6 0.0 copy-start.5
  2.6 4.1 %collective-permute-start = (f32[56,256]{1,0:T(8,128)}, f32[56,256]{1,0:T(8,128)S(1)}, u32[]{:S(2)}, u32[]{:S(2)}) collective-permute-start(f32[56,256]{1,0:T(8,128)} %pack_message.1), channel_id=1, source_target_pairs={{0,16},{4,20},{8,24},{12,28},{16,0},{20,4},{24,8},{28,12},{1,17},{... | collective-permute-start | bytes 172040 | tf_op jit(solution)/shard_map/ppermute | solution.py:408
  6.7 0.0 copy-done.1
  6.7 0.0 copy-done
  6.7 0.0 copy-done.3
  6.7 1.0 %tables.1 = (f32[4,8,256]{2,1,0:T(8,128)S(1)}, f32[16,16,256]{2,1,0:T(8,128)S(1)}, bf16[4,256,256]{2,1,0:T(8,128)(2,1)S(1)}, bf16[4,256,256]{2,1,0:T(8,128)(2,1)...) custom-call(f32[4,256]{1,0:T(4,128)S(1)} %copy-done.3, f32[4,256,256]{2,1,0:T(8,128)S(1)} %copy-done, ...), custom_call_target="tpu_custom_call" | custom-call | flops 268435456 | bytes 4194304 | tf_op jit(solution)/shard_map/tables/pallas_call | solution.py:442
  7.7 2.0 %collective-permute-done = f32[56,256]{1,0:T(8,128)S(1)} collective-permute-done((f32[56,256]{1,0:T(8,128)}, f32[56,256]{1,0:T(8,128)S(1)}, u32[]{:S(2)}, u32[]{:S(2)}) %collective-permute-start) | collective-permute-done | bytes 57376 | tf_op jit(solution)/shard_map/ppermute | solution.py:408
  9.7 0.0 copy-done.5
  9.7 0.0 copy-start.2
  9.7 0.0 copy-start.4
  9.7 2.4 %collective-permute-start.3 = (f32[112,256]{1,0:T(8,128)S(1)}, f32[112,256]{1,0:T(8,128)S(1)}, u32[]{:S(2)}, u32[]{:S(2)}) collective-permute-start(f32[112,256]{1,0:T(8,128)S(1)} %pad_maximum_fusion.refs_0_), channel_id=1, source_target_pairs={{0,12},{4,8},{8,4},{12,0},{16,28},{20,24},{24,20},{28,16},{1,13},{... | collective-permute-start | bytes 344072 | tf_op jit(solution)/shard_map/ppermute | solution.py:408
  12.1 0.9 %collective-permute-start.2 = (f32[112,256]{1,0:T(8,128)S(1)}, f32[112,256]{1,0:T(8,128)S(1)}, u32[]{:S(2)}, u32[]{:S(2)}) collective-permute-start(f32[112,256]{1,0:T(8,128)S(1)} %pad_maximum_fusion.refs_0_), channel_id=1, source_target_pairs={{0,8},{4,12},{8,0},{12,4},{16,24},{20,28},{24,16},{28,20},{1,9},{5... | collective-permute-start | bytes 344072 | tf_op jit(solution)/shard_map/ppermute | solution.py:408
  13.0 0.3 collective-permute-start.1
  13.3 2.3 %pairs.1 = (bf16[16,256,256]{2,1,0:T(8,128)(2,1)S(1)}, bf16[16,256,256]{2,1,0:T(8,128)(2,1)S(1)}) custom-call(bf16[4,256,256]{2,1,0:T(8,128)(2,1)S(1)} %get-tuple-element.28.back_high.refs_8_, bf16[4,256,256]{2,1,0:T(8,128)(2,1)S(1)} %get-tuple-element.29.back_low.refs_9_), custom_call_target="tpu_custom_call" | custom-call | flops 1610612736 | bytes 4194304 | tf_op jit(solution)/shard_map/pairs/pallas_call | solution.py:453
  15.7 0.0 collective-permute-done.3.refs_3_
  15.7 1.3 %collective-permute-done.2.refs_2_ = f32[112,256]{1,0:T(8,128)S(1)} collective-permute-done((f32[112,256]{1,0:T(8,128)S(1)}, f32[112,256]{1,0:T(8,128)S(1)}, u32[]{:S(2)}, u32[]{:S(2)}) %collective-permute-start.2) | collective-permute-done | bytes 114720 | tf_op jit(solution)/shard_map/ppermute | solution.py:408
  17.0 0.8 %collective-permute-done.1.refs_1_ = f32[112,256]{1,0:T(8,128)S(1)} collective-permute-done((f32[112,256]{1,0:T(8,128)S(1)}, f32[112,256]{1,0:T(8,128)S(1)}, u32[]{:S(2)}, u32[]{:S(2)}) %collective-permute-start.1) | collective-permute-done | bytes 114720 | tf_op jit(solution)/shard_map/ppermute | solution.py:408
  17.8 0.0 copy-done.2
  17.8 0.0 copy-done.4
  17.8 18.0 %filter_and_smooth.1 = (f32[16,16,256]{2,1,0:T(8,128)}, f32[16,16,256]{2,1,0:T(8,128)}) custom-call(f32[16,16,256]{2,1,0:T(8,128)S(1)} %copy-done.2, f32[1,256]{1,0:T(1,128)S(1)} %bitcast.1, f32[112,256]{1,0:T(8,128)S(1)} %pad_maximum_fusion.refs_0_, f32[112,256]{1,0:T(8,128)S(1)} %collective-permute-done.1.refs_1_, ...), custom_call_target="tpu_custom_call" | custom-call | tf_op jit(solution)/shard_map/filter_and_smooth/pallas_call | solution.py:478
  (1 shorter events, 0.0 us)
Async XLA Ops:
  0.6 6.1 %copy-start.1 = (f32[4,256,256]{2,1,0:T(8,128)S(1)}, f32[4,256,256]{2,1,0:T(8,128)}, u32[]{:S(2)}) copy-start(f32[4,256,256]{2,1,0:T(8,128)} %back.3) | copy-start | bytes 3145732
  0.6 6.1 %copy-start = (f32[4,256,256]{2,1,0:T(8,128)S(1)}, f32[4,256,256]{2,1,0:T(8,128)}, u32[]{:S(2)}) copy-start(f32[4,256,256]{2,1,0:T(8,128)} %gain.3) | copy-start | bytes 3145732
  0.7 6.1 %copy-start.3 = (f32[4,256]{1,0:T(4,128)S(1)}, f32[4,256]{1,0:T(4,128)}, u32[]{:S(2)}) copy-start(f32[4,256]{1,0:T(4,128)} %diffusivity.1) | copy-start | bytes 12292
  2.6 7.1 %copy-start.5 = (f32[56,256]{1,0:T(8,128)S(1)}, f32[56,256]{1,0:T(8,128)}, u32[]{:S(2)}) copy-start(f32[56,256]{1,0:T(8,128)} %pack_message.1) | copy-start | bytes 172036
  2.6 7.1 %collective-permute-start = (f32[56,256]{1,0:T(8,128)}, f32[56,256]{1,0:T(8,128)S(1)}, u32[]{:S(2)}, u32[]{:S(2)}) collective-permute-start(f32[56,256]{1,0:T(8,128)} %pack_message.1), channel_id=1, source_target_pairs={{0,16},{4,20},{8,24},{12,28},{16,0},{20,4},{24,8},{28,12},{1,17},{... | collective-permute-start | bytes 172040 | tf_op jit(solution)/shard_map/ppermute | solution.py:408
  9.7 8.1 %copy-start.2 = (f32[16,16,256]{2,1,0:T(8,128)S(1)}, f32[16,16,256]{2,1,0:T(8,128)}, u32[]{:S(2)}) copy-start(f32[16,16,256]{2,1,0:T(8,128)} %observations.1) | copy-start | bytes 786436
  9.7 8.0 %copy-start.4 = (f32[256]{0:T(256)S(1)}, f32[256]{0:T(256)}, u32[]{:S(2)}) copy-start(f32[256]{0:T(256)} %param.13) | copy-start | bytes 3076
  9.7 5.9 %collective-permute-start.3 = (f32[112,256]{1,0:T(8,128)S(1)}, f32[112,256]{1,0:T(8,128)S(1)}, u32[]{:S(2)}, u32[]{:S(2)}) collective-permute-start(f32[112,256]{1,0:T(8,128)S(1)} %pad_maximum_fusion.refs_0_), channel_id=1, source_target_pairs={{0,12},{4,8},{8,4},{12,0},{16,28},{20,24},{24,20},{28,16},{1,13},{... | collective-permute-start | bytes 344072 | tf_op jit(solution)/shard_map/ppermute | solution.py:408
  12.1 4.9 %collective-permute-start.2 = (f32[112,256]{1,0:T(8,128)S(1)}, f32[112,256]{1,0:T(8,128)S(1)}, u32[]{:S(2)}, u32[]{:S(2)}) collective-permute-start(f32[112,256]{1,0:T(8,128)S(1)} %pad_maximum_fusion.refs_0_), channel_id=1, source_target_pairs={{0,8},{4,12},{8,0},{12,4},{16,24},{20,28},{24,16},{28,20},{1,9},{5... | collective-permute-start | bytes 344072 | tf_op jit(solution)/shard_map/ppermute | solution.py:408
  13.0 4.8 %collective-permute-start.1 = (f32[112,256]{1,0:T(8,128)S(1)}, f32[112,256]{1,0:T(8,128)S(1)}, u32[]{:S(2)}, u32[]{:S(2)}) collective-permute-start(f32[112,256]{1,0:T(8,128)S(1)} %pad_maximum_fusion.refs_0_), channel_id=1, source_target_pairs={{0,4},{4,0},{8,12},{12,8},{16,20},{20,16},{24,28},{28,24},{1,5},{5... | collective-permute-start | bytes 344072 | tf_op jit(solution)/shard_map/ppermute | solution.py:408

commit v3 on v2

--- a/solution.py
+++ b/solution.py
@@ -11,7 +11,7 @@
 SLOTS = 3
 META = 8
 BF, F32 = jnp.bfloat16, jnp.float32
-VMEM_BYTES = 40 * 2**20
+VMEM_BYTES = 44 * 2**20
 QUADS_BYTES = 2**24
 PACK_VMEM_BYTES = 60 * 2**20
 
@@ -75,11 +75,64 @@
     return tree_sum([weights[k : k + 1] * from_cell(value, s) for k, s in enumerate(shifts)])
 
 
-def tables_kernel(bands, diffusivity, gain, back, one, two, gain_high, gain_low, back_high, back_low):
+def folded_lane(cells, lane):
+    half, rest = lane // (cells // 2), lax.rem(lane, cells // 2)
+    return rest // (GRID // 2) * GRID + lax.rem(rest, GRID // 2) * 2 + half
+
+
+def apply_folded(weights, shifts, value):
+    half = value.shape[1] // 2
+    parts, rolled = (value[:, :half], value[:, half:]), {}
+
+    def moved(part, by):
+        if (part, by) not in rolled:
+            rolled[part, by] = from_cell(parts[part], by)
+        return rolled[part, by]
+
+    out = []
+    for h in (0, 1):
+        terms = []
+        for k, s in enumerate(shifts):
+            down = (s + GRID // 2) // GRID
+            across = h + s - down * GRID
+            terms.append(weights[k : k + 1, h * half : (h + 1) * half] * moved(across % 2, down * (GRID // 2) + across // 2))
+        out.append(tree_sum(terms))
+    return jnp.concatenate(out, 1)
+
+
+def reorder(rows, order):
+    high = rows.astype(BF)
+    rest = rows - high.astype(F32)
+    middle = rest.astype(BF)
+    low = (rest - middle.astype(F32)).astype(BF)
+    return dot(high, order) + (dot(middle, order) + dot(low, order))
+
+
+def folded_rows(value, space):
+    cells = value.shape[0]
+    starts = [r * GRID + h for h in (0, 1) for r in range(cells // GRID)]
+    columns = []
+    for i in range(space.shape[0]):
+        space[i] = value[:, i * 128 : (i + 1) * 128]
+        columns.append(jnp.concatenate([space[i, pl.ds(at, GRID // 2, stride=2), :] for at in starts], 0))
+    return jnp.concatenate(columns, 1)
+
+
+def tables_kernel(
+    bands, diffusivity, gain, back, start, one, two, gain_high, gain_low, next_high, next_low, back_high, back_low, fold, unfold,
+    first_rows, space, natural,
+):
+    cells = diffusivity.shape[1]
+    index = [lax.broadcasted_iota(jnp.int32, (cells, cells), d) for d in (0, 1)]
+    fold[...] = (index[0] == folded_lane(cells, index[1])).astype(F32).astype(BF)
+    unfold[...] = (index[1] == folded_lane(cells, index[0])).astype(F32).astype(BF)
+    unit = (index[0] == index[1]).astype(F32)
     first = stencils(diffusivity[...])
+    natural[...] = jnp.zeros(natural.shape, F32)
     for b in range(bands):
         for k, s in enumerate(SHIFTS):
-            one[b, k : k + 1, :] = first[s][b : b + 1]
+            natural[b * 8 + k : b * 8 + k + 1, :] = first[s][b : b + 1]
+    own_rows = bands * 8
     for b in range(bands):
         for c in range(bands):
             total = {}
@@ -88,10 +141,22 @@
                     term = first[s][c : c + 1] * from_cell(first[r][b : b + 1], s)
                     total[s + r] = total[s + r] + term if s + r in total else term
             for k, s in enumerate(two_step_shifts()):
-                two[b * bands + c, k : k + 1, :] = total[s]
+                at = own_rows + (b * bands + c) * 16 + k
+                natural[at : at + 1, :] = total[s]
+    at = own_rows + bands * bands * 16
+    natural[at : at + 1, :] = start[...]
+    folded = reorder(natural[...], fold[...])
+    one[...] = folded[:own_rows].reshape(one.shape)
+    two[...] = folded[own_rows:at].reshape(two.shape)
+    first_rows[...] = jnp.broadcast_to(folded[at : at + 1], first_rows.shape)
     for b in range(bands):
-        gain_high[b], gain_low[b] = halves(gain[b].T)
-        back_high[b], back_low[b] = halves(back[b].T)
+        weights = natural[b * 8 : b * 8 + 8, :]
+        gain_high[b], gain_low[b] = halves(folded_rows(gain[b], space.at[b, 0]).T)
+        after = apply_stencil(weights, SHIFTS, unit - gain[b])
+        after = folded_rows(after, space.at[b, 1]).T
+        next_high[b], next_low[b] = halves(folded_rows(after, space.at[b, 2]))
+        after = folded_rows(back[b], space.at[b, 3]).T
+        back_high[b], back_low[b] = halves(folded_rows(after, space.at[b, 4]))
 
 
 def pairs_kernel(bands, back_high, back_low, pair_high, pair_low):
@@ -117,7 +182,7 @@
     ]
     for copy in copies:
         copy.start()
-    for copy in copies:
+    for copy in copies[:2]:
         copy.wait()
     lane = lax.broadcasted_iota(jnp.int32, (META, states), 1)
     meta = jnp.zeros((META, states), jnp.int32)
@@ -131,11 +196,6 @@
         meta = put(band_at + t, band[t])
         meta = put(mask_at + t, mask[t])
         meta = put(slot_at + t, count)
-
-        @pl.when((mask[t] > 0) & (count < SLOTS))
-        def _(t=t, at=count):
-            message[pl.ds(at * records, records), :] = observations[t]
-
         count = count + mask[t]
     packed = count > SLOTS
     for p in range(steps // 2):
@@ -154,6 +214,16 @@
         meta = put(oct_own_at + o, ways_own[2 * o] + ways_own[2 * o + 1])
     meta = put(count_at, count)
     message[SLOTS * records :, :] = meta.astype(F32)
+    for copy in copies[2:]:
+        copy.wait()
+    at = jnp.int32(0)
+    for t in range(steps):
+
+        @pl.when((mask[t] > 0) & (at < SLOTS))
+        def _(t=t, at=at):
+            message[pl.ds(pl.multiple_of(at * records, 8), records), :] = observations[t]
+
+        at = at + mask[t]
 
     for slot in range(SLOTS):
 
@@ -199,12 +269,11 @@
     fields,
     pieces,
     observations,
-    start,
     *refs,
 ):
     parts, refs = refs[:pieces], refs[pieces:]
-    (one, two, gain_high, gain_low, back_high, back_low, pair_high, pair_low), refs = refs[:8], refs[8:]
-    (filtered_far, smoothed_far, held, smoothed, out_sem), refs = refs[:5], refs[5:]
+    (one, two, gain_high, gain_low, next_high, next_low, back_high, back_low, fold, unfold, first_rows), refs = refs[:11], refs[11:]
+    (pair_high, pair_low, filtered_far, smoothed_far, held, outward, out_sem), refs = refs[:7], refs[7:]
     (inbox, meta, table, delta, pushed, sem), quads = refs[:6], refs[6:]
     steps, records, states = observations.shape
     per = steps // 4
@@ -237,13 +306,13 @@
     copy.wait()
 
     def step(b, x):
-        return apply_stencil(one[b], SHIFTS, x)
+        return apply_folded(one[b], SHIFTS, x)
 
     def two_steps(pair, x):
-        return apply_stencil(two[pair], two_step_shifts(), x)
-
-    def innovation(b, difference):
-        return rows_product(difference, gain_high[b], gain_low[b])
+        return apply_folded(two[pair], two_step_shifts(), x)
+
+    def observed_step(b, x, y):
+        return rows_product(x, next_high[b], next_low[b]) + rows_product(y, gain_high[b], gain_low[b])
 
     def back(b, r):
         return rows_product(r, back_high[b], back_low[b])
@@ -295,13 +364,14 @@
             held[at + k + 1] = x
             return x
 
-        def corrected(b, k, p, packed=False):
+        def corrected(b, k, x, packed=False):
             slot = lax.rem(table[block, slot_at + 4 * q + k], SLOTS)
             sent = inbox[pl.ds(pl.multiple_of(first + slot * records, 8), records), :]
             y = jnp.where(packed, 0.0, jnp.where(own, observations[4 * q + k], sent))
-            change = innovation(b, y - p)
-            delta[at + k] = change
-            return change
+            p, x = step(b, x), observed_step(b, x, y)
+            delta[at + k] = x - p
+            held[at + k + 1] = x
+            return x
 
         def one_seen(k, x):
             b = four(band_at, block, q)
@@ -311,9 +381,8 @@
                 x = keep(1, two_steps(early, x))
             if k % 2:
                 x = keep(k - 1, step(b[k - 1], x))
-            p = step(b[k], x)
-            change = corrected(b[k], k, p)
-            x = keep(k, p + change)
+            x = corrected(b[k], k, x)
+            change = delta[at + k]
             if k % 2 == 0:
                 x = keep(k + 1, step(b[k + 1], x))
             if k < 2:
@@ -332,14 +401,23 @@
             packed = (table[block, count_at] > SLOTS) & jnp.logical_not(own)
             prepare(block, q)
             for k in range(4):
-                p = step(b[k], x)
-                x = keep(k, lax.cond(m[k] > 0, lambda p, k=k: p + corrected(b[k], k, p, packed), lambda p: p, p))
+                x = lax.cond(
+                    m[k] > 0,
+                    lambda x, k=k: corrected(b[k], k, x, packed),
+                    lambda x, k=k: keep(k, step(b[k], x)),
+                    x,
+                )
             r = jnp.zeros_like(x)
             for k in (3, 2, 1):
                 r = back(b[k - 1], added(m[k], at + k, r))
-            r_sent = inbox[pl.ds(pl.multiple_of(first + records, 8), records), :]
-            pushed[block * per + q] = jnp.where(packed & (q == 0), r + r_sent, r)
-            return keep(3, jnp.where(packed & (q == per - 1), x + inbox[pl.ds(first, records), :], x))
+            pushed[block * per + q] = r
+
+            def add_sent(slot):
+                sent = inbox[pl.ds(pl.multiple_of(first + slot * records, 8), records), :]
+                return lambda x: x + reorder(sent, fold[...])
+
+            pushed[block * per + q] = lax.cond(packed & (q == 0), add_sent(1), lambda r: r, r)
+            return keep(3, lax.cond(packed & (q == per - 1), add_sent(0), lambda x: x, x))
 
         return lax.switch(
             table[block, jnp.where(own, quad_own_at, quad_at) + q],
@@ -358,7 +436,7 @@
     def filter_block(block, x):
         return lax.fori_loop(0, per // 2, functools.partial(filter_oct, block), x)
 
-    held[0] = jnp.broadcast_to(start[...], (records, states))
+    held[0] = first_rows[...]
     x = lax.fori_loop(0, me + 1, filter_block, held[0])
     own_bands = [four(band_at, me, q) for q in range(per)]
     own_masks = [four(mask_at, me, q) for q in range(per)]
@@ -368,10 +446,9 @@
             seen = own_masks[q][k] + own_masks[q][k + 1] > 0
             held[at + 1] = jnp.where(seen, held[at + 1], step(own_bands[q][k], held[at]))
     outs = [
-        pltpu.make_async_copy(a, b, out_sem.at[i])
-        for i, (a, b) in enumerate(((held.at[pl.ds(me * steps + 1, steps)], filtered_far), (smoothed, smoothed_far)))
+        [pltpu.make_async_copy(outward.at[k, i], far.at[:, k], out_sem.at[k, i]) for i, far in enumerate((filtered_far, smoothed_far))]
+        for k in range(4)
     ]
-    outs[0].start()
     lax.fori_loop(me + 1, devices, filter_block, x)
 
     def smooth_block(i, r):
@@ -383,19 +460,23 @@
 
     r = lax.fori_loop(0, devices - 1 - me, smooth_block, jnp.zeros((records, states), F32))
 
-    def smooth(q, k, e):
-        smoothed[q * 4 + k] = held[me * steps + q * 4 + k + 1] + e
-        return added(own_masks[q][k], me * steps + q * 4 + k, e)
-
-    after = [None] * per
+    def leave(k, after):
+        before = [held[me * steps + q * 4 + k + 1] for q in range(per)]
+        rows_out = jnp.concatenate(before + [x + e for x, e in zip(before, after)], 0)
+        outward[k] = reorder(rows_out, unfold[...]).reshape(outward.shape[1:])
+        for copy in outs[k]:
+            copy.start()
+        return [added(own_masks[q][k], me * steps + q * 4 + k, after[q]) for q in range(per)]
+
+    after, ends = [None] * per, [None] * per
     for q in reversed(range(per)):
         after[q] = r
-        r = smooth(q, 0, over_quad(me, q, r) + pushed[me * per + q])
+        ends[q] = over_quad(me, q, r) + pushed[me * per + q]
+        r = added(own_masks[q][0], me * steps + q * 4, ends[q])
+    leave(0, ends)
     for k in (3, 2, 1):
-        for q in range(per):
-            after[q] = smooth(q, k, back(own_bands[q][k], after[q]))
-    outs[1].start()
-    for copy in outs:
+        after = leave(k, [back(own_bands[q][k], after[q]) for q in range(per)])
+    for copy in sum(outs, []):
         copy.wait()
 
 
@@ -441,13 +522,20 @@
     def make_tables():
         return pl.pallas_call(
             functools.partial(tables_kernel, bands),
-            out_shape=[shape((bands, 8, states), F32), shape((bands * bands, 16, states), F32)] + [matrix(bands)] * 4,
-            in_specs=[whole()] * 3,
-            out_specs=[whole()] * 6,
+            out_shape=[shape((bands, 8, states), F32), shape((bands * bands, 16, states), F32)]
+            + [matrix(bands)] * 6
+            + [shape((states, states), BF)] * 2
+            + [shape((records, states), F32)],
+            in_specs=[whole()] * 4,
+            out_specs=[whole()] * 11,
+            scratch_shapes=[
+                pltpu.VMEM((bands, 5, states // 128, states, 128), F32),
+                pltpu.VMEM((bands * 8 + bands * bands * 16 + 8, states), F32),
+            ],
             compiler_params=params,
             cost_estimate=cost(2**28),
             name="tables",
-        )(diffusivity, gain, back)
+        )(diffusivity, gain, back, initial_mean[None, :])
 
     def make_pairs(back_high, back_low):
         return pl.pallas_call(
@@ -471,19 +559,19 @@
         pieces = xor_round(held, low, width, devices)
         fields = [(low, 1 << width)] + fields
     tables = make_tables() if tables is None else tables
-    tables = [*tables, *make_pairs(*tables[4:6])]
-    out = shape((steps, records, states), F32)
+    tables = [*tables, *make_pairs(*tables[6:8])]
+    out = shape((steps // 4, 4, records, states), F32)
     quads = devices * steps // 4
     deep = quads * states * states * 4 <= QUADS_BYTES
-    return pl.pallas_call(
+    filtered, smoothed = pl.pallas_call(
         functools.partial(main_kernel, bands, devices, fields, len(pieces)),
         out_shape=[out, out],
-        in_specs=[whole()] * (2 + len(pieces) + len(tables)),
+        in_specs=[whole()] * (1 + len(pieces) + len(tables)),
         out_specs=[whole(pltpu.HBM)] * 2,
         scratch_shapes=[
             pltpu.VMEM((devices * steps + 1, records, states), F32),
-            pltpu.VMEM((steps, records, states), F32),
-            pltpu.SemaphoreType.DMA((2,)),
+            pltpu.VMEM((4, 2, steps // 4, records, states), F32),
+            pltpu.SemaphoreType.DMA((4, 2)),
             pltpu.VMEM((devices * rows, states), F32),
             pltpu.VMEM((devices, states), jnp.int32),
             pltpu.SMEM((devices, states), jnp.int32),
@@ -494,7 +582,8 @@
         + [pltpu.VMEM((quads, states, states), BF)] * (2 * deep),
         compiler_params=params,
         name="filter_and_smooth",
-    )(observations, initial_mean[None, :], *pieces, *tables)
+    )(observations, *pieces, *tables)
+    return filtered.reshape(observations.shape), smoothed.reshape(observations.shape)
 
 
 def solution(mesh):

time: 36.2 us -> 35.6 us (0.983)
  waiting for transfers between devices: 4.09 us -> 2.33 us
  Pallas kernels: 23.3 us -> 24.5 us
    pallas_call x1, Pallas kernels: 0.99 us -> 2.93 us  [make_tables(): pl.pallas_call(functools.partial(tables_kernel, bands), out_shape=[shape(...]
    ppermute x4, waiting for transfers between devices: 4.09 us -> 2.33 us  [xor_round(): lax.ppermute(held, 'tm', [(i, i ^ k << low) for i in range(devices)])]
    pallas_call x1, Pallas kernels: 18 us -> 17.4 us  [shards(): pl.pallas_call(functools.partial(main_kernel, bands, devices, fields, len...]
  transfers between devices with their start and end apart: 4 -> 4, of which waited for: 3 -> 3; matrix products, arithmetic and copies ran while one was open for 0% -> 0% of each run, Pallas kernels for 9% -> 15%
where the time goes in v3:
time: 35.6 us; the launch traced here: 35.2 us
  Pallas kernels  24.5 us (69%)
  starting transfers between devices  7.65 us (21%)
  waiting for transfers between devices  2.33 us (7%)
  between operations  0.71 us (2%)
    pallas_call x1, Pallas kernels, shards(): pl.pallas_call(functools.partial(main_kernel, bands, devices, fields, len...  17.4 us
    ppermute x4, starting transfers between devices, xor_round(): lax.ppermute(held, 'tm', [(i, i ^ k << low) for i in range(devices)])  7.65 us
    pallas_call x1, Pallas kernels, make_tables(): pl.pallas_call(functools.partial(tables_kernel, bands), out_shape=[shape(...  2.93 us
    pallas_call x1, Pallas kernels, make_pairs(): pl.pallas_call(functools.partial(pairs_kernel, bands), out_shape=[matrix(...  2.39 us
    ppermute x4, waiting for transfers between devices, xor_round(): lax.ppermute(held, 'tm', [(i, i ^ k << low) for i in range(devices)])  2.33 us
    pallas_call x1, Pallas kernels, shards(): pl.pallas_call(functools.partial(pack_kernel, bands), out_shape=shape((ro...  1.76 us
  transfers between devices with their start and end apart: 4, of which 3 were waited for; matrix products, arithmetic and copies ran while one was open for 0% of the time, Pallas kernels for 15%

profile of v3, /device:TPU:0, one launch (start us, length us, event | category | flops | bytes accessed | tf_op | source)
XLA Modules:
  0.0 35.2 jit_solution(14383055783954024124)
XLA Ops:
  0.6 0.0 copy-start.1
  0.6 0.0 copy-start
  0.7 0.0 copy-start.3
  0.7 0.0 copy-start.4
  0.7 1.8 %pack_message.1 = f32[56,256]{1,0:T(8,128)} custom-call(s32[16]{0:T(128)} %band_far.1, s32[16]{0:T(128)} %mask_far.1, f32[16,16,256]{2,1,0:T(8,128)} %observations.1, f32[4,256]{1,0:T(4,128)} %diffusivity.1, f32[4,256,256]{2,1,0:T(8,128)} %gain.3, f32[4,256,256]{2,1,0:T(8,128)} %back.3), custom_call_target="tpu_custom_call" | custom-call | tf_op jit(solution)/shard_map/pack_message/pallas_call | solution.py:500
  2.4 0.0 copy-start.5
  2.5 4.1 %collective-permute-start = (f32[56,256]{1,0:T(8,128)}, f32[56,256]{1,0:T(8,128)S(1)}, u32[]{:S(2)}, u32[]{:S(2)}) collective-permute-start(f32[56,256]{1,0:T(8,128)} %pack_message.1), channel_id=1, source_target_pairs={{0,16},{4,20},{8,24},{12,28},{16,0},{20,4},{24,8},{28,12},{1,17},{... | collective-permute-start | bytes 172040 | tf_op jit(solution)/shard_map/ppermute | solution.py:489
  6.6 0.0 copy-done.1
  6.6 0.0 copy-done
  6.6 0.0 copy-done.3
  6.6 0.0 copy-done.4
  6.6 2.9 %tables.1 = (f32[4,8,256]{2,1,0:T(8,128)S(1)}, f32[16,16,256]{2,1,0:T(8,128)S(1)}, bf16[4,256,256]{2,1,0:T(8,128)(2,1)S(1)}, bf16[4,256,256]{2,1,0:T(8,128)(2,1)...) custom-call(f32[4,256]{1,0:T(4,128)S(1)} %copy-done.3, ...), custom_call_target="tpu_custom_call" | custom-call | flops 268435456 | bytes 4194304 | tf_op jit(solution)/shard_map/tables/pallas_call | solution.py:523
  9.5 0.0 collective-permute-done
  9.5 0.0 copy-done.5
  9.5 0.0 copy-start.2
  9.6 2.6 %collective-permute-start.3 = (f32[112,256]{1,0:T(8,128)S(1)}, f32[112,256]{1,0:T(8,128)S(1)}, u32[]{:S(2)}, u32[]{:S(2)}) collective-permute-start(f32[112,256]{1,0:T(8,128)S(1)} %pad_maximum_fusion.refs_0_), channel_id=1, source_target_pairs={{0,12},{4,8},{8,4},{12,0},{16,28},{20,24},{24,20},{28,16},{1,13},{... | collective-permute-start | bytes 344072 | tf_op jit(solution)/shard_map/ppermute | solution.py:489
  12.1 0.7 %collective-permute-start.2 = (f32[112,256]{1,0:T(8,128)S(1)}, f32[112,256]{1,0:T(8,128)S(1)}, u32[]{:S(2)}, u32[]{:S(2)}) collective-permute-start(f32[112,256]{1,0:T(8,128)S(1)} %pad_maximum_fusion.refs_0_), channel_id=1, source_target_pairs={{0,8},{4,12},{8,0},{12,4},{16,24},{20,28},{24,16},{28,20},{1,9},{5... | collective-permute-start | bytes 344072 | tf_op jit(solution)/shard_map/ppermute | solution.py:489
  12.8 0.3 collective-permute-start.1
  13.1 2.4 %pairs.1 = (bf16[16,256,256]{2,1,0:T(8,128)(2,1)S(1)}, bf16[16,256,256]{2,1,0:T(8,128)(2,1)S(1)}) custom-call(bf16[4,256,256]{2,1,0:T(8,128)(2,1)S(1)} %get-tuple-element.47.back_high.refs_10_, bf16[4,256,256]{2,1,0:T(8,128)(2,1)S(1)} %get-tuple-element.48.back_low.refs_11_), custom_call_target="tpu_custom_call" | custom-call | flops 1610612736 | bytes 4194304 | tf_op jit(solution)/shard_map/pairs/pallas_call | solution.py:541
  15.5 1.0 %collective-permute-done.3.refs_3_ = f32[112,256]{1,0:T(8,128)S(1)} collective-permute-done((f32[112,256]{1,0:T(8,128)S(1)}, f32[112,256]{1,0:T(8,128)S(1)}, u32[]{:S(2)}, u32[]{:S(2)}) %collective-permute-start.3) | collective-permute-done | bytes 114720 | tf_op jit(solution)/shard_map/ppermute | solution.py:489
  16.5 1.2 %collective-permute-done.2.refs_2_ = f32[112,256]{1,0:T(8,128)S(1)} collective-permute-done((f32[112,256]{1,0:T(8,128)S(1)}, f32[112,256]{1,0:T(8,128)S(1)}, u32[]{:S(2)}, u32[]{:S(2)}) %collective-permute-start.2) | collective-permute-done | bytes 114720 | tf_op jit(solution)/shard_map/ppermute | solution.py:489
  17.7 0.1 collective-permute-done.1.refs_1_
  17.8 0.0 copy-done.2
  17.8 17.4 %filter_and_smooth.1 = (f32[4,4,16,256]{3,2,1,0:T(8,128)}, f32[4,4,16,256]{3,2,1,0:T(8,128)}) custom-call(f32[16,16,256]{2,1,0:T(8,128)S(1)} %copy-done.2, f32[112,256]{1,0:T(8,128)S(1)} %pad_maximum_fusion.refs_0_, f32[112,256]{1,0:T(8,128)S(1)} %collective-permute-done.1.refs_1_, f32[112,256]{1,0:T(8,128)S(1)} %collective-permute-done.2.refs_2_, ...), custom_call_target="tpu_custom_call" | custom-call | tf_op jit(solution)/shard_map/filter_and_smooth/pallas_call | solution.py:566
  (1 shorter events, 0.0 us)
Async XLA Ops:
  0.6 5.9 %copy-start.1 = (f32[4,256,256]{2,1,0:T(8,128)S(1)}, f32[4,256,256]{2,1,0:T(8,128)}, u32[]{:S(2)}) copy-start(f32[4,256,256]{2,1,0:T(8,128)} %back.3) | copy-start | bytes 3145732
  0.6 5.9 %copy-start = (f32[4,256,256]{2,1,0:T(8,128)S(1)}, f32[4,256,256]{2,1,0:T(8,128)}, u32[]{:S(2)}) copy-start(f32[4,256,256]{2,1,0:T(8,128)} %gain.3) | copy-start | bytes 3145732
  0.7 5.9 %copy-start.3 = (f32[4,256]{1,0:T(4,128)S(1)}, f32[4,256]{1,0:T(4,128)}, u32[]{:S(2)}) copy-start(f32[4,256]{1,0:T(4,128)} %diffusivity.1) | copy-start | bytes 12292
  0.7 5.9 %copy-start.4 = (f32[256]{0:T(256)S(1)}, f32[256]{0:T(256)}, u32[]{:S(2)}) copy-start(f32[256]{0:T(256)} %param.13) | copy-start | bytes 3076
  2.4 7.1 %copy-start.5 = (f32[56,256]{1,0:T(8,128)S(1)}, f32[56,256]{1,0:T(8,128)}, u32[]{:S(2)}) copy-start(f32[56,256]{1,0:T(8,128)} %pack_message.1) | copy-start | bytes 172036
  2.5 7.1 %collective-permute-start = (f32[56,256]{1,0:T(8,128)}, f32[56,256]{1,0:T(8,128)S(1)}, u32[]{:S(2)}, u32[]{:S(2)}) collective-permute-start(f32[56,256]{1,0:T(8,128)} %pack_message.1), channel_id=1, source_target_pairs={{0,16},{4,20},{8,24},{12,28},{16,0},{20,4},{24,8},{28,12},{1,17},{... | collective-permute-start | bytes 172040 | tf_op jit(solution)/shard_map/ppermute | solution.py:489
  9.5 8.3 %copy-start.2 = (f32[16,16,256]{2,1,0:T(8,128)S(1)}, f32[16,16,256]{2,1,0:T(8,128)}, u32[]{:S(2)}) copy-start(f32[16,16,256]{2,1,0:T(8,128)} %observations.1) | copy-start | bytes 786436
  9.6 7.0 %collective-permute-start.3 = (f32[112,256]{1,0:T(8,128)S(1)}, f32[112,256]{1,0:T(8,128)S(1)}, u32[]{:S(2)}, u32[]{:S(2)}) collective-permute-start(f32[112,256]{1,0:T(8,128)S(1)} %pad_maximum_fusion.refs_0_), channel_id=1, source_target_pairs={{0,12},{4,8},{8,4},{12,0},{16,28},{20,24},{24,20},{28,16},{1,13},{... | collective-permute-start | bytes 344072 | tf_op jit(solution)/shard_map/ppermute | solution.py:489
  12.1 5.6 %collective-permute-start.2 = (f32[112,256]{1,0:T(8,128)S(1)}, f32[112,256]{1,0:T(8,128)S(1)}, u32[]{:S(2)}, u32[]{:S(2)}) collective-permute-start(f32[112,256]{1,0:T(8,128)S(1)} %pad_maximum_fusion.refs_0_), channel_id=1, source_target_pairs={{0,8},{4,12},{8,0},{12,4},{16,24},{20,28},{24,16},{28,20},{1,9},{5... | collective-permute-start | bytes 344072 | tf_op jit(solution)/shard_map/ppermute | solution.py:489
  12.8 5.0 %collective-permute-start.1 = (f32[112,256]{1,0:T(8,128)S(1)}, f32[112,256]{1,0:T(8,128)S(1)}, u32[]{:S(2)}, u32[]{:S(2)}) collective-permute-start(f32[112,256]{1,0:T(8,128)S(1)} %pad_maximum_fusion.refs_0_), channel_id=1, source_target_pairs={{0,4},{4,0},{8,12},{12,8},{16,20},{20,16},{24,28},{28,24},{1,5},{5... | collective-permute-start | bytes 344072 | tf_op jit(solution)/shard_map/ppermute | solution.py:489

commit v4 on v3

--- a/solution.py
+++ b/solution.py
@@ -101,11 +101,13 @@
 
 
 def reorder(rows, order):
+    m = rows.shape[0]
     high = rows.astype(BF)
     rest = rows - high.astype(F32)
     middle = rest.astype(BF)
     low = (rest - middle.astype(F32)).astype(BF)
-    return dot(high, order) + (dot(middle, order) + dot(low, order))
+    parts = dot(jnp.concatenate([high, middle, low], 0), order)
+    return parts[:m] + (parts[m : 2 * m] + parts[2 * m :])
 
 
 def folded_rows(value, space):
@@ -263,7 +265,25 @@
         message[records : 2 * records, :] = lax.fori_loop(0, steps, backward, zeros)
 
 
-def main_kernel(
+def main_kernel(*args):
+    records, states = args[4].shape[1:]
+    small = [[pltpu.ACC(i)((records, states), F32) for i in (0, 1)] for _ in range(4)]
+    large = [pltpu.ACC(i)((states // 2, states), F32) for i in (0, 1)]
+    pl.run_scoped(functools.partial(filter_and_smooth, *args), small, large, pltpu.ACC(0)((4 * records, states), F32))
+
+
+def times_many(products, sums):
+    for i, (rows, high, low) in enumerate(products):
+        rows_high, rows_low = halves(rows)
+        pltpu.matmul_push_rhs(high, i % 2, 0)
+        pltpu.matmul_push_rhs(low, i % 2, 1)
+        pltpu.matmul_acc_lhs(sums[i][0], rows_high, load_staged_rhs=i % 2)
+        pltpu.matmul_acc_lhs(sums[i][1], rows_high, load_staged_rhs=i % 2)
+        pltpu.matmul_acc_lhs(sums[i][0], rows_low)
+    return [pltpu.matmul_pop(a) + pltpu.matmul_pop(b) for a, b in sums[: len(products)]]
+
+
+def filter_and_smooth(
     bands,
     devices,
     fields,
@@ -271,9 +291,28 @@
     observations,
     *refs,
 ):
+    refs, (small, large, many) = refs[:-3], refs[-3:]
+
+    def rows_product(rows, high, low):
+        return times_many([(rows, high, low)], small)[0]
+
+    def reorder(rows, order, sums=None):
+        sums = sums or [many if rows.shape[0] == many.shape[0] else small[0][0]]
+        each = rows.shape[0] // len(sums)
+        for i, into in enumerate(sums):
+            pltpu.matmul_push_rhs(order, 0, i)
+            part = rows[i * each : (i + 1) * each]
+            high = part.astype(BF)
+            rest = part - high.astype(F32)
+            middle = rest.astype(BF)
+            pltpu.matmul_acc_lhs(into, (rest - middle.astype(F32)).astype(BF), load_staged_rhs=0)
+            pltpu.matmul_acc_lhs(into, middle)
+            pltpu.matmul_acc_lhs(into, high)
+        return jnp.concatenate([pltpu.matmul_pop(into) for into in sums], 0)
+
     parts, refs = refs[:pieces], refs[pieces:]
     (one, two, gain_high, gain_low, next_high, next_low, back_high, back_low, fold, unfold, first_rows), refs = refs[:11], refs[11:]
-    (pair_high, pair_low, filtered_far, smoothed_far, held, outward, out_sem), refs = refs[:7], refs[7:]
+    (pair_high, pair_low, filtered_far, smoothed_far, held, outward, ready, after, ends, out_sem), refs = refs[:10], refs[10:]
     (inbox, meta, table, delta, pushed, sem), quads = refs[:6], refs[6:]
     steps, records, states = observations.shape
     per = steps // 4
@@ -312,7 +351,7 @@
         return apply_folded(two[pair], two_step_shifts(), x)
 
     def observed_step(b, x, y):
-        return rows_product(x, next_high[b], next_low[b]) + rows_product(y, gain_high[b], gain_low[b])
+        return sum(times_many([(y, gain_high[b], gain_low[b]), (x, next_high[b], next_low[b])], small))
 
     def back(b, r):
         return rows_product(r, back_high[b], back_low[b])
@@ -329,11 +368,26 @@
         return [table[block, at + 4 * q + k] for k in range(4)]
 
     def prepare(block, q):
-        if quads:
-            right, left = pairs(block, q)
-            high, low = pair_high[left], pair_low[left]
-            product = dot(high, pair_high[right]) + (dot(low, pair_high[right]) + dot(high, pair_low[right]))
-            quads[0][block * per + q], quads[1][block * per + q] = halves(product)
+        if not quads:
+            return lambda: None
+        right, left = pairs(block, q)
+        high, low = pair_high[left], pair_low[left]
+        n = states // 2
+        for i in (0, 1):
+            pltpu.matmul_push_rhs(pair_high[right], 0, i)
+            pltpu.matmul_push_rhs(pair_low[right], 1, i)
+            into = large[i]
+            h, l = high[i * n : (i + 1) * n], low[i * n : (i + 1) * n]
+            pltpu.matmul_acc_lhs(into, h, load_staged_rhs=0)
+            pltpu.matmul_acc_lhs(into, l)
+            pltpu.matmul_acc_lhs(into, h, load_staged_rhs=1)
+
+        def finish():
+            for i in (0, 1):
+                rows = pl.ds(i * n, n)
+                quads[0][block * per + q, rows, :], quads[1][block * per + q, rows, :] = halves(pltpu.matmul_pop(large[i]))
+
+        return finish
 
     def over_quad(block, q, r):
         if quads:
@@ -347,10 +401,11 @@
     def plain(block, q, x):
         early, late = pairs(block, q)
         at = (block * per + q) * 4 + 1
-        prepare(block, q)
+        finish = prepare(block, q)
         pushed[block * per + q] = jnp.zeros_like(x)
         x = two_steps(early, x)
         held[at + 1] = x
+        finish()
         x = two_steps(late, x)
         held[at + 3] = x
         return x
@@ -376,7 +431,7 @@
         def one_seen(k, x):
             b = four(band_at, block, q)
             early, late = pairs(block, q)
-            prepare(block, q)
+            finish = prepare(block, q)
             if k >= 2:
                 x = keep(1, two_steps(early, x))
             if k % 2:
@@ -394,12 +449,13 @@
             else:
                 change = back_two(early, change if k == 2 else back(b[2], change))
             pushed[block * per + q] = change
+            finish()
             return x
 
         def any_seen(x):
             b, m = four(band_at, block, q), four(mask_at, block, q)
             packed = (table[block, count_at] > SLOTS) & jnp.logical_not(own)
-            prepare(block, q)
+            prepare(block, q)()
             for k in range(4):
                 x = lax.cond(
                     m[k] > 0,
@@ -445,38 +501,68 @@
             at = me * steps + q * 4 + k
             seen = own_masks[q][k] + own_masks[q][k + 1] > 0
             held[at + 1] = jnp.where(seen, held[at + 1], step(own_bands[q][k], held[at]))
-    outs = [
-        [pltpu.make_async_copy(outward.at[k, i], far.at[:, k], out_sem.at[k, i]) for i, far in enumerate((filtered_far, smoothed_far))]
-        for k in range(4)
-    ]
+    outs = [pltpu.make_async_copy(outward.at[k], smoothed_far.at[:, k], out_sem.at[k]) for k in range(4)]
+    outs.append(pltpu.make_async_copy(ready, filtered_far, out_sem.at[4]))
     lax.fori_loop(me + 1, devices, filter_block, x)
 
-    def smooth_block(i, r):
-        block = devices - 1 - i
-        for q in reversed(range(per)):
-            r = over_quad(block, q, r) + pushed[block * per + q]
-            r = added(table[block, mask_at + 4 * q], block * steps + 4 * q, r)
-        return r
-
-    r = lax.fori_loop(0, devices - 1 - me, smooth_block, jnp.zeros((records, states), F32))
+    def smooth_quad(block, q, r, gains):
+        after[q] = r
+        e = gains(block, q, r) + pushed[block * per + q]
+        ends[q] = e
+        return added(table[block, mask_at + 4 * q], block * steps + 4 * q, e)
+
+    def smooth_all(gains):
+        def smooth_block(i, r):
+            for q in reversed(range(per)):
+                r = smooth_quad(devices - 1 - i, q, r, gains)
+            return r
+
+        lax.fori_loop(0, devices - me, smooth_block, jnp.zeros((records, states), F32))
+
+    def smooth_staged():
+        high_sum, low_sum = small[0]
+
+        def stage(quad):
+            pltpu.matmul_push_rhs(quads[0][quad], 0, 0)
+            pltpu.matmul_push_rhs(quads[1][quad], 0, 1)
+
+        def multiply(high, low):
+            pltpu.matmul_acc_lhs(high_sum, high, load_staged_rhs=0)
+            pltpu.matmul_acc_lhs(low_sum, high, load_staged_rhs=0)
+            pltpu.matmul_acc_lhs(high_sum, low)
+
+        def gains(block, q, r):
+            multiply(*halves(r))
+            stage(jnp.maximum(block * per + q - 1, 0))
+            return pltpu.matmul_pop(high_sum) + pltpu.matmul_pop(low_sum)
+
+        stage(devices * per - 1)
+        smooth_all(gains)
+        none = jnp.zeros((records, states), BF)
+        multiply(none, none)
+        ends[per] = pltpu.matmul_pop(high_sum) + pltpu.matmul_pop(low_sum)
+
+    if quads:
+        smooth_staged()
+    else:
+        smooth_all(over_quad)
+
+    own_held = held[pl.ds(me * steps + 1, steps)].reshape(steps * records, states)
+    ready[...] = reorder(own_held, unfold[...], large).reshape(ready.shape)
+    outs[4].start()
 
     def leave(k, after):
-        before = [held[me * steps + q * 4 + k + 1] for q in range(per)]
-        rows_out = jnp.concatenate(before + [x + e for x, e in zip(before, after)], 0)
+        rows_out = jnp.concatenate([held[me * steps + q * 4 + k + 1] + after[q] for q in range(per)], 0)
         outward[k] = reorder(rows_out, unfold[...]).reshape(outward.shape[1:])
-        for copy in outs[k]:
-            copy.start()
+        outs[k].start()
         return [added(own_masks[q][k], me * steps + q * 4 + k, after[q]) for q in range(per)]
 
-    after, ends = [None] * per, [None] * per
-    for q in reversed(range(per)):
-        after[q] = r
-        ends[q] = over_quad(me, q, r) + pushed[me * per + q]
-        r = added(own_masks[q][0], me * steps + q * 4, ends[q])
-    leave(0, ends)
+    leave(0, [ends[q] for q in range(per)])
+    r = [after[q] for q in range(per)]
     for k in (3, 2, 1):
-        after = leave(k, [back(own_bands[q][k], after[q]) for q in range(per)])
-    for copy in sum(outs, []):
+        b = [own_bands[q][k] for q in range(per)]
+        r = leave(k, times_many([(r[q], back_high[b[q]], back_low[b[q]]) for q in range(per)], small))
+    for copy in outs:
         copy.wait()
 
 
@@ -570,8 +656,11 @@
         out_specs=[whole(pltpu.HBM)] * 2,
         scratch_shapes=[
             pltpu.VMEM((devices * steps + 1, records, states), F32),
-            pltpu.VMEM((4, 2, steps // 4, records, states), F32),
-            pltpu.SemaphoreType.DMA((4, 2)),
+            pltpu.VMEM((4, steps // 4, records, states), F32),
+            pltpu.VMEM((steps // 4, 4, records, states), F32),
+            pltpu.VMEM((steps // 4, records, states), F32),
+            pltpu.VMEM((steps // 4 + 1, records, states), F32),
+            pltpu.SemaphoreType.DMA((5,)),
             pltpu.VMEM((devices * rows, states), F32),
             pltpu.VMEM((devices, states), jnp.int32),
             pltpu.SMEM((devices, states), jnp.int32),

time: 35.6 us -> 35.1 us (0.986); the launches traced: 35.2 us -> 35.5 us
    pallas_call x1, Pallas kernels: 17.4 us -> 17.8 us  [shards(): pl.pallas_call(functools.partial(main_kernel, bands, devices, fields, len...]
  transfers between devices with their start and end apart: 4 -> 4, of which waited for: 3 -> 4; matrix products, arithmetic and copies ran while one was open for 0% -> 0% of each run, Pallas kernels for 15% -> 15%
where the time goes in v4:
time: 35.1 us; the launch traced here: 35.5 us
  Pallas kernels  24.7 us (70%)
  starting transfers between devices  7.66 us (22%)
  waiting for transfers between devices  2.36 us (7%)
  between operations  0.71 us (2%)
    pallas_call x1, Pallas kernels, shards(): pl.pallas_call(functools.partial(main_kernel, bands, devices, fields, len...  17.8 us
    ppermute x4, starting transfers between devices, xor_round(): lax.ppermute(held, 'tm', [(i, i ^ k << low) for i in range(devices)])  7.66 us
    pallas_call x1, Pallas kernels, make_tables(): pl.pallas_call(functools.partial(tables_kernel, bands), out_shape=[shape(...  2.77 us
    pallas_call x1, Pallas kernels, make_pairs(): pl.pallas_call(functools.partial(pairs_kernel, bands), out_shape=[matrix(...  2.39 us
    ppermute x4, waiting for transfers between devices, xor_round(): lax.ppermute(held, 'tm', [(i, i ^ k << low) for i in range(devices)])  2.36 us
    pallas_call x1, Pallas kernels, shards(): pl.pallas_call(functools.partial(pack_kernel, bands), out_shape=shape((ro...  1.76 us
  transfers between devices with their start and end apart: 4, of which 4 were waited for; matrix products, arithmetic and copies ran while one was open for 0% of the time, Pallas kernels for 15%

profile of v4, /device:TPU:0, one launch (start us, length us, event | category | flops | bytes accessed | tf_op | source)
XLA Modules:
  0.0 35.5 jit_solution(14019324756308823987)
XLA Ops:
  0.6 0.0 copy-start.1
  0.6 0.0 copy-start
  0.7 0.0 copy-start.3
  0.7 0.0 copy-start.4
  0.7 1.8 %pack_message.1 = f32[56,256]{1,0:T(8,128)} custom-call(s32[16]{0:T(128)} %band_far.1, s32[16]{0:T(128)} %mask_far.1, f32[16,16,256]{2,1,0:T(8,128)} %args_0_.4, f32[4,256]{1,0:T(4,128)} %diffusivity.1, f32[4,256,256]{2,1,0:T(8,128)} %gain.3, f32[4,256,256]{2,1,0:T(8,128)} %back.3), custom_call_target="tpu_custom_call" | custom-call | tf_op jit(solution)/shard_map/pack_message/pallas_call | solution.py:586
  2.4 0.0 copy-start.5
  2.4 4.1 %collective-permute-start = (f32[56,256]{1,0:T(8,128)}, f32[56,256]{1,0:T(8,128)S(1)}, u32[]{:S(2)}, u32[]{:S(2)}) collective-permute-start(f32[56,256]{1,0:T(8,128)} %pack_message.1), channel_id=1, source_target_pairs={{0,16},{4,20},{8,24},{12,28},{16,0},{20,4},{24,8},{28,12},{1,17},{... | collective-permute-start | bytes 172040 | tf_op jit(solution)/shard_map/ppermute | solution.py:575
  6.6 0.0 copy-done.1
  6.6 0.0 copy-done
  6.6 0.0 copy-done.3
  6.6 0.0 copy-done.4
  6.6 2.8 %tables.1 = (f32[4,8,256]{2,1,0:T(8,128)S(1)}, f32[16,16,256]{2,1,0:T(8,128)S(1)}, bf16[4,256,256]{2,1,0:T(8,128)(2,1)S(1)}, bf16[4,256,256]{2,1,0:T(8,128)(2,1)...) custom-call(f32[4,256]{1,0:T(4,128)S(1)} %copy-done.3, ...), custom_call_target="tpu_custom_call" | custom-call | flops 268435456 | bytes 4194304 | tf_op jit(solution)/shard_map/tables/pallas_call | solution.py:609
  9.3 0.2 collective-permute-done
  9.5 0.0 copy-done.5
  9.5 0.0 copy-start.2
  9.6 2.4 %collective-permute-start.3 = (f32[112,256]{1,0:T(8,128)S(1)}, f32[112,256]{1,0:T(8,128)S(1)}, u32[]{:S(2)}, u32[]{:S(2)}) collective-permute-start(f32[112,256]{1,0:T(8,128)S(1)} %pad_maximum_fusion.args_1_), channel_id=1, source_target_pairs={{0,12},{4,8},{8,4},{12,0},{16,28},{20,24},{24,20},{28,16},{1,13},{... | collective-permute-start | bytes 344072 | tf_op jit(solution)/shard_map/ppermute | solution.py:575
  12.0 0.8 %collective-permute-start.2 = (f32[112,256]{1,0:T(8,128)S(1)}, f32[112,256]{1,0:T(8,128)S(1)}, u32[]{:S(2)}, u32[]{:S(2)}) collective-permute-start(f32[112,256]{1,0:T(8,128)S(1)} %pad_maximum_fusion.args_1_), channel_id=1, source_target_pairs={{0,8},{4,12},{8,0},{12,4},{16,24},{20,28},{24,16},{28,20},{1,9},{5... | collective-permute-start | bytes 344072 | tf_op jit(solution)/shard_map/ppermute | solution.py:575
  12.8 0.3 collective-permute-start.1
  13.1 2.4 %pairs.1 = (bf16[16,256,256]{2,1,0:T(8,128)(2,1)S(1)}, bf16[16,256,256]{2,1,0:T(8,128)(2,1)S(1)}) custom-call(bf16[4,256,256]{2,1,0:T(8,128)(2,1)S(1)} %get-tuple-element.47.back_high.args_11_, bf16[4,256,256]{2,1,0:T(8,128)(2,1)S(1)} %get-tuple-element.48.back_low.args_12_), custom_call_target="tpu_custom_call" | custom-call | flops 1610612736 | bytes 4194304 | tf_op jit(solution)/shard_map/pairs/pallas_call | solution.py:627
  15.5 0.8 %collective-permute-done.3.args_4_ = f32[112,256]{1,0:T(8,128)S(1)} collective-permute-done((f32[112,256]{1,0:T(8,128)S(1)}, f32[112,256]{1,0:T(8,128)S(1)}, u32[]{:S(2)}, u32[]{:S(2)}) %collective-permute-start.3) | collective-permute-done | bytes 114720 | tf_op jit(solution)/shard_map/ppermute | solution.py:575
  16.4 1.1 %collective-permute-done.2.args_3_ = f32[112,256]{1,0:T(8,128)S(1)} collective-permute-done((f32[112,256]{1,0:T(8,128)S(1)}, f32[112,256]{1,0:T(8,128)S(1)}, u32[]{:S(2)}, u32[]{:S(2)}) %collective-permute-start.2) | collective-permute-done | bytes 114720 | tf_op jit(solution)/shard_map/ppermute | solution.py:575
  17.5 0.2 collective-permute-done.1.args_2_
  17.7 0.0 copy-done.2
  17.7 17.8 %filter_and_smooth.1 = (f32[4,4,16,256]{3,2,1,0:T(8,128)}, f32[4,4,16,256]{3,2,1,0:T(8,128)}) custom-call(f32[16,16,256]{2,1,0:T(8,128)S(1)} %copy-done.2, f32[112,256]{1,0:T(8,128)S(1)} %pad_maximum_fusion.args_1_, f32[112,256]{1,0:T(8,128)S(1)} %collective-permute-done.1.args_2_, f32[112,256]{1,0:T(8,128)S(1)} %collective-permute-done.2.args_3_, ...), custom_call_target="tpu_custom_call" | custom-call | tf_op jit(solution)/shard_map/filter_and_smooth/pallas_call | solution.py:652
  (1 shorter events, 0.0 us)
Async XLA Ops:
  0.6 5.9 %copy-start.1 = (f32[4,256,256]{2,1,0:T(8,128)S(1)}, f32[4,256,256]{2,1,0:T(8,128)}, u32[]{:S(2)}) copy-start(f32[4,256,256]{2,1,0:T(8,128)} %back.3) | copy-start | bytes 3145732
  0.6 5.9 %copy-start = (f32[4,256,256]{2,1,0:T(8,128)S(1)}, f32[4,256,256]{2,1,0:T(8,128)}, u32[]{:S(2)}) copy-start(f32[4,256,256]{2,1,0:T(8,128)} %gain.3) | copy-start | bytes 3145732
  0.7 5.9 %copy-start.3 = (f32[4,256]{1,0:T(4,128)S(1)}, f32[4,256]{1,0:T(4,128)}, u32[]{:S(2)}) copy-start(f32[4,256]{1,0:T(4,128)} %diffusivity.1) | copy-start | bytes 12292
  0.7 5.9 %copy-start.4 = (f32[256]{0:T(256)S(1)}, f32[256]{0:T(256)}, u32[]{:S(2)}) copy-start(f32[256]{0:T(256)} %param.13) | copy-start | bytes 3076
  2.4 7.1 %copy-start.5 = (f32[56,256]{1,0:T(8,128)S(1)}, f32[56,256]{1,0:T(8,128)}, u32[]{:S(2)}) copy-start(f32[56,256]{1,0:T(8,128)} %pack_message.1) | copy-start | bytes 172036
  2.4 7.1 %collective-permute-start = (f32[56,256]{1,0:T(8,128)}, f32[56,256]{1,0:T(8,128)S(1)}, u32[]{:S(2)}, u32[]{:S(2)}) collective-permute-start(f32[56,256]{1,0:T(8,128)} %pack_message.1), channel_id=1, source_target_pairs={{0,16},{4,20},{8,24},{12,28},{16,0},{20,4},{24,8},{28,12},{1,17},{... | collective-permute-start | bytes 172040 | tf_op jit(solution)/shard_map/ppermute | solution.py:575
  9.5 8.1 %copy-start.2 = (f32[16,16,256]{2,1,0:T(8,128)S(1)}, f32[16,16,256]{2,1,0:T(8,128)}, u32[]{:S(2)}) copy-start(f32[16,16,256]{2,1,0:T(8,128)} %args_0_.4) | copy-start | bytes 786436
  9.6 6.8 %collective-permute-start.3 = (f32[112,256]{1,0:T(8,128)S(1)}, f32[112,256]{1,0:T(8,128)S(1)}, u32[]{:S(2)}, u32[]{:S(2)}) collective-permute-start(f32[112,256]{1,0:T(8,128)S(1)} %pad_maximum_fusion.args_1_), channel_id=1, source_target_pairs={{0,12},{4,8},{8,4},{12,0},{16,28},{20,24},{24,20},{28,16},{1,13},{... | collective-permute-start | bytes 344072 | tf_op jit(solution)/shard_map/ppermute | solution.py:575
  12.0 5.6 %collective-permute-start.2 = (f32[112,256]{1,0:T(8,128)S(1)}, f32[112,256]{1,0:T(8,128)S(1)}, u32[]{:S(2)}, u32[]{:S(2)}) collective-permute-start(f32[112,256]{1,0:T(8,128)S(1)} %pad_maximum_fusion.args_1_), channel_id=1, source_target_pairs={{0,8},{4,12},{8,0},{12,4},{16,24},{20,28},{24,16},{28,20},{1,9},{5... | collective-permute-start | bytes 344072 | tf_op jit(solution)/shard_map/ppermute | solution.py:575
  12.8 4.9 %collective-permute-start.1 = (f32[112,256]{1,0:T(8,128)S(1)}, f32[112,256]{1,0:T(8,128)S(1)}, u32[]{:S(2)}, u32[]{:S(2)}) collective-permute-start(f32[112,256]{1,0:T(8,128)S(1)} %pad_maximum_fusion.args_1_), channel_id=1, source_target_pairs={{0,4},{4,0},{8,12},{12,8},{16,20},{20,16},{24,28},{28,24},{1,5},{5... | collective-permute-start | bytes 344072 | tf_op jit(solution)/shard_map/ppermute | solution.py:575

commit v5 on v4

--- a/solution.py
+++ b/solution.py
@@ -272,7 +272,7 @@
     pl.run_scoped(functools.partial(filter_and_smooth, *args), small, large, pltpu.ACC(0)((4 * records, states), F32))
 
 
-def times_many(products, sums):
+def times_many(products, sums, then=None):
     for i, (rows, high, low) in enumerate(products):
         rows_high, rows_low = halves(rows)
         pltpu.matmul_push_rhs(high, i % 2, 0)
@@ -280,6 +280,8 @@
         pltpu.matmul_acc_lhs(sums[i][0], rows_high, load_staged_rhs=i % 2)
         pltpu.matmul_acc_lhs(sums[i][1], rows_high, load_staged_rhs=i % 2)
         pltpu.matmul_acc_lhs(sums[i][0], rows_low)
+    if then is not None:
+        pltpu.matmul_push_rhs(then, 0, 0)
     return [pltpu.matmul_pop(a) + pltpu.matmul_pop(b) for a, b in sums[: len(products)]]
 
 
@@ -296,11 +298,12 @@
     def rows_product(rows, high, low):
         return times_many([(rows, high, low)], small)[0]
 
-    def reorder(rows, order, sums=None):
+    def reorder(rows, order, sums=None, staged=False):
         sums = sums or [many if rows.shape[0] == many.shape[0] else small[0][0]]
         each = rows.shape[0] // len(sums)
         for i, into in enumerate(sums):
-            pltpu.matmul_push_rhs(order, 0, i)
+            if not staged:
+                pltpu.matmul_push_rhs(order, 0, i)
             part = rows[i * each : (i + 1) * each]
             high = part.astype(BF)
             rest = part - high.astype(F32)
@@ -551,9 +554,9 @@
     ready[...] = reorder(own_held, unfold[...], large).reshape(ready.shape)
     outs[4].start()
 
-    def leave(k, after):
+    def leave(k, after, staged=False):
         rows_out = jnp.concatenate([held[me * steps + q * 4 + k + 1] + after[q] for q in range(per)], 0)
-        outward[k] = reorder(rows_out, unfold[...]).reshape(outward.shape[1:])
+        outward[k] = reorder(rows_out, unfold[...], staged=staged).reshape(outward.shape[1:])
         outs[k].start()
         return [added(own_masks[q][k], me * steps + q * 4 + k, after[q]) for q in range(per)]
 
@@ -561,7 +564,7 @@
     r = [after[q] for q in range(per)]
     for k in (3, 2, 1):
         b = [own_bands[q][k] for q in range(per)]
-        r = leave(k, times_many([(r[q], back_high[b[q]], back_low[b[q]]) for q in range(per)], small))
+        r = leave(k, times_many([(r[q], back_high[b[q]], back_low[b[q]]) for q in range(per)], small, unfold[...]), True)
     for copy in outs:
         copy.wait()
 

time: 35.1 us -> 35.2 us (level); the launches traced: 35.5 us -> 35.1 us
  Pallas kernels: 24.7 us -> 24.3 us
where the time goes in v5:
time: 35.2 us; the launch traced here: 35.1 us
  Pallas kernels  24.3 us (69%)
  starting transfers between devices  7.66 us (22%)
  waiting for transfers between devices  2.36 us (7%)
  between operations  0.71 us (2%)
    pallas_call x1, Pallas kernels, shards(): pl.pallas_call(functools.partial(main_kernel, bands, devices, fields, len...  17.4 us
    ppermute x4, starting transfers between devices, xor_round(): lax.ppermute(held, 'tm', [(i, i ^ k << low) for i in range(devices)])  7.66 us
    pallas_call x1, Pallas kernels, make_tables(): pl.pallas_call(functools.partial(tables_kernel, bands), out_shape=[shape(...  2.77 us
    pallas_call x1, Pallas kernels, make_pairs(): pl.pallas_call(functools.partial(pairs_kernel, bands), out_shape=[matrix(...  2.39 us
    ppermute x4, waiting for transfers between devices, xor_round(): lax.ppermute(held, 'tm', [(i, i ^ k << low) for i in range(devices)])  2.36 us
    pallas_call x1, Pallas kernels, shards(): pl.pallas_call(functools.partial(pack_kernel, bands), out_shape=shape((ro...  1.76 us
  transfers between devices with their start and end apart: 4, of which 4 were waited for; matrix products, arithmetic and copies ran while one was open for 0% of the time, Pallas kernels for 15%

profile of v5, /device:TPU:0, one launch (start us, length us, event | category | flops | bytes accessed | tf_op | source)
XLA Modules:
  0.0 35.1 jit_solution(14019324756308823987)
XLA Ops:
  0.6 0.0 copy-start.1
  0.6 0.0 copy-start
  0.7 0.0 copy-start.3
  0.7 0.0 copy-start.4
  0.7 1.8 %pack_message.1 = f32[56,256]{1,0:T(8,128)} custom-call(s32[16]{0:T(128)} %band_far.1, s32[16]{0:T(128)} %mask_far.1, f32[16,16,256]{2,1,0:T(8,128)} %args_0_.4, f32[4,256]{1,0:T(4,128)} %diffusivity.1, f32[4,256,256]{2,1,0:T(8,128)} %gain.3, f32[4,256,256]{2,1,0:T(8,128)} %back.3), custom_call_target="tpu_custom_call" | custom-call | tf_op jit(solution)/shard_map/pack_message/pallas_call | solution.py:589
  2.4 0.0 copy-start.5
  2.4 4.1 %collective-permute-start = (f32[56,256]{1,0:T(8,128)}, f32[56,256]{1,0:T(8,128)S(1)}, u32[]{:S(2)}, u32[]{:S(2)}) collective-permute-start(f32[56,256]{1,0:T(8,128)} %pack_message.1), channel_id=1, source_target_pairs={{0,16},{4,20},{8,24},{12,28},{16,0},{20,4},{24,8},{28,12},{1,17},{... | collective-permute-start | bytes 172040 | tf_op jit(solution)/shard_map/ppermute | solution.py:578
  6.6 0.0 copy-done.1
  6.6 0.0 copy-done
  6.6 0.0 copy-done.3
  6.6 0.0 copy-done.4
  6.6 2.8 %tables.1 = (f32[4,8,256]{2,1,0:T(8,128)S(1)}, f32[16,16,256]{2,1,0:T(8,128)S(1)}, bf16[4,256,256]{2,1,0:T(8,128)(2,1)S(1)}, bf16[4,256,256]{2,1,0:T(8,128)(2,1)...) custom-call(f32[4,256]{1,0:T(4,128)S(1)} %copy-done.3, ...), custom_call_target="tpu_custom_call" | custom-call | flops 268435456 | bytes 4194304 | tf_op jit(solution)/shard_map/tables/pallas_call | solution.py:612
  9.3 0.2 collective-permute-done
  9.5 0.0 copy-done.5
  9.5 0.0 copy-start.2
  9.6 2.4 %collective-permute-start.3 = (f32[112,256]{1,0:T(8,128)S(1)}, f32[112,256]{1,0:T(8,128)S(1)}, u32[]{:S(2)}, u32[]{:S(2)}) collective-permute-start(f32[112,256]{1,0:T(8,128)S(1)} %pad_maximum_fusion.args_1_), channel_id=1, source_target_pairs={{0,12},{4,8},{8,4},{12,0},{16,28},{20,24},{24,20},{28,16},{1,13},{... | collective-permute-start | bytes 344072 | tf_op jit(solution)/shard_map/ppermute | solution.py:578
  12.0 0.8 %collective-permute-start.2 = (f32[112,256]{1,0:T(8,128)S(1)}, f32[112,256]{1,0:T(8,128)S(1)}, u32[]{:S(2)}, u32[]{:S(2)}) collective-permute-start(f32[112,256]{1,0:T(8,128)S(1)} %pad_maximum_fusion.args_1_), channel_id=1, source_target_pairs={{0,8},{4,12},{8,0},{12,4},{16,24},{20,28},{24,16},{28,20},{1,9},{5... | collective-permute-start | bytes 344072 | tf_op jit(solution)/shard_map/ppermute | solution.py:578
  12.8 0.3 collective-permute-start.1
  13.1 2.4 %pairs.1 = (bf16[16,256,256]{2,1,0:T(8,128)(2,1)S(1)}, bf16[16,256,256]{2,1,0:T(8,128)(2,1)S(1)}) custom-call(bf16[4,256,256]{2,1,0:T(8,128)(2,1)S(1)} %get-tuple-element.47.back_high.args_11_, bf16[4,256,256]{2,1,0:T(8,128)(2,1)S(1)} %get-tuple-element.48.back_low.args_12_), custom_call_target="tpu_custom_call" | custom-call | flops 1610612736 | bytes 4194304 | tf_op jit(solution)/shard_map/pairs/pallas_call | solution.py:630
  15.5 0.8 %collective-permute-done.3.args_4_ = f32[112,256]{1,0:T(8,128)S(1)} collective-permute-done((f32[112,256]{1,0:T(8,128)S(1)}, f32[112,256]{1,0:T(8,128)S(1)}, u32[]{:S(2)}, u32[]{:S(2)}) %collective-permute-start.3) | collective-permute-done | bytes 114720 | tf_op jit(solution)/shard_map/ppermute | solution.py:578
  16.4 1.2 %collective-permute-done.2.args_3_ = f32[112,256]{1,0:T(8,128)S(1)} collective-permute-done((f32[112,256]{1,0:T(8,128)S(1)}, f32[112,256]{1,0:T(8,128)S(1)}, u32[]{:S(2)}, u32[]{:S(2)}) %collective-permute-start.2) | collective-permute-done | bytes 114720 | tf_op jit(solution)/shard_map/ppermute | solution.py:578
  17.5 0.2 collective-permute-done.1.args_2_
  17.7 0.0 copy-done.2
  17.7 17.4 %filter_and_smooth.1 = (f32[4,4,16,256]{3,2,1,0:T(8,128)}, f32[4,4,16,256]{3,2,1,0:T(8,128)}) custom-call(f32[16,16,256]{2,1,0:T(8,128)S(1)} %copy-done.2, f32[112,256]{1,0:T(8,128)S(1)} %pad_maximum_fusion.args_1_, f32[112,256]{1,0:T(8,128)S(1)} %collective-permute-done.1.args_2_, f32[112,256]{1,0:T(8,128)S(1)} %collective-permute-done.2.args_3_, ...), custom_call_target="tpu_custom_call" | custom-call | tf_op jit(solution)/shard_map/filter_and_smooth/pallas_call | solution.py:655
  (1 shorter events, 0.0 us)
Async XLA Ops:
  0.6 5.9 %copy-start.1 = (f32[4,256,256]{2,1,0:T(8,128)S(1)}, f32[4,256,256]{2,1,0:T(8,128)}, u32[]{:S(2)}) copy-start(f32[4,256,256]{2,1,0:T(8,128)} %back.3) | copy-start | bytes 3145732
  0.6 5.9 %copy-start = (f32[4,256,256]{2,1,0:T(8,128)S(1)}, f32[4,256,256]{2,1,0:T(8,128)}, u32[]{:S(2)}) copy-start(f32[4,256,256]{2,1,0:T(8,128)} %gain.3) | copy-start | bytes 3145732
  0.7 5.9 %copy-start.3 = (f32[4,256]{1,0:T(4,128)S(1)}, f32[4,256]{1,0:T(4,128)}, u32[]{:S(2)}) copy-start(f32[4,256]{1,0:T(4,128)} %diffusivity.1) | copy-start | bytes 12292
  0.7 5.9 %copy-start.4 = (f32[256]{0:T(256)S(1)}, f32[256]{0:T(256)}, u32[]{:S(2)}) copy-start(f32[256]{0:T(256)} %param.13) | copy-start | bytes 3076
  2.4 7.1 %copy-start.5 = (f32[56,256]{1,0:T(8,128)S(1)}, f32[56,256]{1,0:T(8,128)}, u32[]{:S(2)}) copy-start(f32[56,256]{1,0:T(8,128)} %pack_message.1) | copy-start | bytes 172036
  2.4 7.1 %collective-permute-start = (f32[56,256]{1,0:T(8,128)}, f32[56,256]{1,0:T(8,128)S(1)}, u32[]{:S(2)}, u32[]{:S(2)}) collective-permute-start(f32[56,256]{1,0:T(8,128)} %pack_message.1), channel_id=1, source_target_pairs={{0,16},{4,20},{8,24},{12,28},{16,0},{20,4},{24,8},{28,12},{1,17},{... | collective-permute-start | bytes 172040 | tf_op jit(solution)/shard_map/ppermute | solution.py:578
  9.5 8.1 %copy-start.2 = (f32[16,16,256]{2,1,0:T(8,128)S(1)}, f32[16,16,256]{2,1,0:T(8,128)}, u32[]{:S(2)}) copy-start(f32[16,16,256]{2,1,0:T(8,128)} %args_0_.4) | copy-start | bytes 786436
  9.6 6.8 %collective-permute-start.3 = (f32[112,256]{1,0:T(8,128)S(1)}, f32[112,256]{1,0:T(8,128)S(1)}, u32[]{:S(2)}, u32[]{:S(2)}) collective-permute-start(f32[112,256]{1,0:T(8,128)S(1)} %pad_maximum_fusion.args_1_), channel_id=1, source_target_pairs={{0,12},{4,8},{8,4},{12,0},{16,28},{20,24},{24,20},{28,16},{1,13},{... | collective-permute-start | bytes 344072 | tf_op jit(solution)/shard_map/ppermute | solution.py:578
  12.0 5.6 %collective-permute-start.2 = (f32[112,256]{1,0:T(8,128)S(1)}, f32[112,256]{1,0:T(8,128)S(1)}, u32[]{:S(2)}, u32[]{:S(2)}) collective-permute-start(f32[112,256]{1,0:T(8,128)S(1)} %pad_maximum_fusion.args_1_), channel_id=1, source_target_pairs={{0,8},{4,12},{8,0},{12,4},{16,24},{20,28},{24,16},{28,20},{1,9},{5... | collective-permute-start | bytes 344072 | tf_op jit(solution)/shard_map/ppermute | solution.py:578
  12.8 4.9 %collective-permute-start.1 = (f32[112,256]{1,0:T(8,128)S(1)}, f32[112,256]{1,0:T(8,128)S(1)}, u32[]{:S(2)}, u32[]{:S(2)}) collective-permute-start(f32[112,256]{1,0:T(8,128)S(1)} %pad_maximum_fusion.args_1_), channel_id=1, source_target_pairs={{0,4},{4,0},{8,12},{12,8},{16,20},{20,16},{24,28},{28,24},{1,5},{5... | collective-permute-start | bytes 344072 | tf_op jit(solution)/shard_map/ppermute | solution.py:578
